TPU v7x, 256 devices: a whole 4x4x8 slice. The times are simulated.
256 devices in a mesh: dp: 32 (over y_hi, z, core), blk: 4 (over x), uly: 2 (over y_lo).
Axes of the slice: x: 4, y: 4 (y_hi: 2, y_lo: 2; y = y_hi * 2 + y_lo), z: 8, core: 2. Of those that a mesh axis runs over, the one named last changes fastest.
Arguments:
- img_query: bfloat16 [32, 1024, 2432], P('dp', ('blk', 'uly')), may hold values from -6 to 6
- img_key: bfloat16 [32, 1024, 2432], P('dp', ('blk', 'uly')), may hold values from -6 to 6
- img_value: bfloat16 [32, 1024, 2432], P('dp', ('blk', 'uly')), may hold values from -6 to 6
- img_cotangent: bfloat16 [32, 1024, 2432], P('dp', ('blk', 'uly')), may hold values from -6 to 6
- txt_query: bfloat16 [32, 32, 2432], P('dp', None, 'uly'), may hold values from -6 to 6
- txt_key: bfloat16 [32, 32, 2432], P('dp', None, 'uly'), may hold values from -6 to 6
- txt_value: bfloat16 [32, 32, 2432], P('dp', None, 'uly'), may hold values from -6 to 6
- txt_cotangent: bfloat16 [32, 32, 2432], P('dp', None, 'uly'), may hold values from -6 to 6
- img_gate: bfloat16 [32, 2432], P('dp'), may hold values from -6 to 6
- txt_gate: bfloat16 [32, 2432], P('dp'), may hold values from -6 to 6
- conditioning: bfloat16 [32, 2432], P('dp'), may hold values from -6 to 6
- norm_gains: float32 [4, 64], replicated, may hold values from 0.1 to 1.9
Outputs:
- img_query_grad: bfloat16 [32, 1024, 2432], P('dp', ('blk', 'uly'))
- img_key_grad: bfloat16 [32, 1024, 2432], P('dp', ('blk', 'uly'))
- img_value_grad: bfloat16 [32, 1024, 2432], P('dp', ('blk', 'uly'))
- txt_query_grad: bfloat16 [32, 32, 2432], P('dp', None, 'uly')
- txt_key_grad: bfloat16 [32, 32, 2432], P('dp', None, 'uly')
- txt_value_grad: bfloat16 [32, 32, 2432], P('dp', None, 'uly')
- modulation_grad: float32 [2432, 2432], P('blk', 'uly')
- txt_gate_grad: float32 [32, 2432], P('dp', 'uly')
All inputs are finite; a program needn't handle non-finite values.
Results may differ from a plain program's by a relative error of at most 0.025.
Values may be sent and summed in bfloat16 or wider, within the bound.
No kernel may reach another device: no remote copies, remote signals or barrier semaphores. Data moves between devices by JAX's collectives and lax.ppermute only.
A program may use at most 192 MiB of HBM per device.

v0:
```python
import functools

import jax
import jax.numpy as jnp
from jax import lax
from jax.experimental import pallas as pl
from jax.experimental.pallas import tpu as pltpu
from jax.sharding import PartitionSpec as P

HEAD = 64
PAIR = 2 * HEAD
EPS = 1e-06
SLOTS = 5
QUERY_STEPS = 3
TEXT_ROWS = 48
GATE_ROW = SLOTS * TEXT_ROWS
VMEM = 56 * 2**20
f32 = jnp.float32
bf16 = jnp.bfloat16


def head_of(dest, slot, half_heads):
    place = (dest // 2) * SLOTS + slot
    return (dest % 2) * half_heads + place if place < half_heads else None


def matmul(left, right):
    return jnp.dot(left, right, preferred_element_type=f32)


def matmul_nt(left, right):
    return lax.dot_general(left, right, (((1,), (1,)), ((), ())), preferred_element_type=f32)


def split_two(wide):
    high = wide.astype(bf16)
    return high, (wide - high.astype(f32)).astype(bf16)


def split_three(wide):
    high = wide.astype(bf16)
    rest = wide - high.astype(f32)
    middle = rest.astype(bf16)
    return high, middle, (rest - middle.astype(f32)).astype(bf16)


def half_means(wide, averager):
    return matmul(jnp.concatenate(split_two(wide), 1), averager)


def pack_kernel(
    half_heads,
    chunks,
    place_ref,
    iq_ref,
    ik_ref,
    iv_ref,
    ic_ref,
    tq_ref,
    tk_ref,
    tv_ref,
    tc_ref,
    ig_ref,
    tg_ref,
    *out_refs,
):
    send_refs, (text_ref, gate_ref) = out_refs[:-2], out_refs[-2:]

    def columns(ref, head):
        return ref[:, head * HEAD : (head + 1) * HEAD]

    rows = iq_ref.shape[0]
    for slots, send_ref in zip(chunks, send_refs):
        for dest in range(send_ref.shape[0]):
            for position, slot in enumerate(slots):
                head = head_of(dest, slot, half_heads)
                for pair, (first, second) in enumerate(((iq_ref, ik_ref), (iv_ref, ic_ref))):
                    tile = (
                        jnp.zeros((rows, PAIR), bf16)
                        if head is None
                        else jnp.concatenate([columns(first, head), columns(second, head)], 1)
                    )
                    start = (2 * position + pair) * rows
                    send_ref[dest, start : start + rows, :] = tile
    place = place_ref[0]
    for device in range(send_refs[0].shape[0]):

        @pl.when(place == device)
        def _():
            for slot in range(SLOTS):
                head = head_of(device, slot, half_heads)
                local = None if head is None else head - (device % 2) * half_heads
                for pair, (first, second) in enumerate(((tq_ref, tk_ref), (tv_ref, tc_ref))):
                    tile = (
                        jnp.zeros((first.shape[0], PAIR), bf16)
                        if local is None
                        else jnp.concatenate([columns(first, local), columns(second, local)], 1)
                    )
                    text_ref[:, (2 * slot + pair) * PAIR : (2 * slot + pair + 1) * PAIR] = tile
                for row, ref in enumerate((ig_ref, tg_ref)):
                    gate = jnp.zeros((1, HEAD), bf16) if head is None else columns(ref, head)
                    gate = gate.astype(f32)
                    gate_ref[slot, row : row + 1, :] = jnp.concatenate([gate, gate], 1)


def attend_kernel(count, in_ref, text_ref, gain_ref, gate_ref, out_ref, pay_ref, sums_ref):
    step = pl.program_id(0)
    devices, tile_rows = in_ref.shape[0], in_ref.shape[1] // 2
    rows, txt = devices * tile_rows, text_ref.shape[0]
    total_rows = rows + txt
    row_at = lax.broadcasted_iota(jnp.int32, (2 * PAIR, PAIR), 0)
    lane_at = lax.broadcasted_iota(jnp.int32, (2 * PAIR, PAIR), 1)
    averager = jnp.where((row_at % PAIR) // HEAD == lane_at // HEAD, 1.0 / HEAD, 0.0).astype(bf16)

    raw = jnp.concatenate(
        [in_ref[:, :tile_rows, :].reshape(rows, PAIR), text_ref[:, :PAIR]], 0
    ).astype(f32)
    value_cotan = jnp.concatenate(
        [in_ref[:, tile_rows:, :].reshape(rows, PAIR), text_ref[:, PAIR:]], 0
    )
    gain = jnp.concatenate(
        [
            jnp.broadcast_to(gain_ref[0:1, :], (rows, PAIR)),
            jnp.broadcast_to(gain_ref[1:2, :], (txt, PAIR)),
        ],
        0,
    )
    inverse = lax.rsqrt(half_means(raw * raw, averager) + EPS)
    normed = (raw * inverse * gain).astype(bf16)
    queries, keys = normed[:, :HEAD], normed[:, HEAD:]
    scaled_queries = queries * jnp.asarray(0.125, bf16)
    values_ones = jnp.concatenate([value_cotan[:, :HEAD], jnp.ones((total_rows, HEAD), bf16)], 1)
    keys_zeros = jnp.concatenate([keys, jnp.zeros((total_rows, HEAD), bf16)], 1)
    cotan = value_cotan[:, HEAD:].astype(f32)
    gate = jnp.concatenate(
        [
            jnp.broadcast_to(gate_ref[0, 0:1, :HEAD], (rows, HEAD)),
            jnp.broadcast_to(gate_ref[0, 1:2, :HEAD], (txt, HEAD)),
        ],
        0,
    )
    upstream = (cotan * gate).astype(bf16).astype(f32)

    size = total_rows // QUERY_STEPS
    lane = lax.broadcasted_iota(jnp.int32, (size, PAIR), 1)
    ones = jnp.ones((2 * HEAD, PAIR), bf16)
    zeros = jnp.zeros((size, HEAD), bf16)
    query_grads = []
    value_key_grad = img_sum = txt_sum = None
    for part in range(QUERY_STEPS):
        at = slice(part * size, (part + 1) * size)
        exponent = jnp.exp(matmul_nt(scaled_queries[at], keys)).astype(bf16)
        weighted = matmul(exponent, values_ones)
        over_total = 1.0 / weighted[:, HEAD:]
        attention = (weighted[:, :HEAD] * over_total).astype(bf16).astype(f32)
        scaled = (upstream[at] * over_total).astype(bf16)
        delta = matmul(jnp.concatenate(split_two(scaled.astype(f32) * attention), 1), ones)
        delta_high, delta_low = split_two(delta)
        extended = jnp.where(
            lane < HEAD,
            jnp.concatenate([scaled, zeros], 1),
            jnp.where(
                lane == HEAD,
                -delta_high,
                jnp.where(lane == HEAD + 1, -delta_low, jnp.zeros_like(delta_low)),
            ),
        )
        prob_grad = matmul_nt(extended, values_ones)
        score_grad = exponent * prob_grad.astype(bf16)
        query_grads.append(matmul(score_grad, keys_zeros))
        term = jnp.concatenate(
            [matmul(scaled.T, exponent), matmul(queries[at].T, score_grad)], 0
        )
        value_key_grad = term if value_key_grad is None else value_key_grad + term
        gated = cotan[at] * attention
        img_rows = min(max(rows - part * size, 0), size)
        if img_rows > 0:
            term = jnp.sum(gated[:img_rows], 0, keepdims=True)
            img_sum = term if img_sum is None else img_sum + term
        if img_rows < size:
            term = jnp.sum(gated[img_rows:], 0, keepdims=True)
            txt_sum = term if txt_sum is None else txt_sum + term
    value_key_grad = value_key_grad.T
    lane = lax.broadcasted_iota(jnp.int32, (total_rows, PAIR), 1)
    scaled = jnp.where(lane < HEAD, jnp.concatenate(query_grads, 0), value_key_grad) * (gain * 0.125)
    mean = half_means(raw * scaled, averager)
    pair_grad = (inverse * scaled - raw * (inverse * inverse * inverse) * mean).astype(bf16)
    value_grad = value_key_grad[:, :HEAD].astype(bf16)

    start = pl.multiple_of(step * tile_rows, tile_rows)
    out_ref[:, pl.ds(start, tile_rows), :] = pair_grad[:rows].reshape(devices, tile_rows, PAIR)
    tiled = value_grad[:rows].reshape(devices, tile_rows, HEAD)
    half = tile_rows // 2
    for head in range(count):

        @pl.when(step == head)
        def _():
            begin = (count + head // 2) * tile_rows
            if head % 2 == 1:
                out_ref[:, begin : begin + tile_rows, HEAD:] = tiled
            elif head < count - 1:
                out_ref[:, begin : begin + tile_rows, :HEAD] = tiled
            else:
                out_ref[:, begin : begin + half, :] = jnp.concatenate(
                    [tiled[:, :half], tiled[:, half:]], 2
                )

    text_grad = value_grad[rows:]
    text_tile = jnp.concatenate(
        [pair_grad[rows:], jnp.concatenate([text_grad[: txt // 2], text_grad[txt // 2 :]], 1)], 0
    )
    start = pl.multiple_of(step * TEXT_ROWS, 16)
    for dest in range(pay_ref.shape[0]):
        pay_ref[dest, pl.ds(start, TEXT_ROWS), :] = text_tile
    sums_ref[pl.ds(step, 1), :] = jnp.concatenate([img_sum, txt_sum], 1)

    @pl.when(step == count - 1)
    def _():
        sums = sums_ref[0:SLOTS, :]
        tail = pay_ref.shape[1] - GATE_ROW - 3 * SLOTS
        packed = jnp.concatenate(
            [part.astype(f32) for part in split_three(sums)] + [jnp.zeros((tail, PAIR), f32)], 0
        ).astype(bf16)
        for dest in range(pay_ref.shape[0]):
            pay_ref[dest, GATE_ROW:, :] = packed


def text_kernel(half_heads, pay_ref, tq_ref, tk_ref, tv_ref, tg_ref, row_ref):
    txt = tq_ref.shape[0]
    blocks = pay_ref.shape[0]
    for block in range(blocks):
        packed = pay_ref[block, GATE_ROW:, :].astype(f32)
        sums = packed[:SLOTS] + packed[SLOTS : 2 * SLOTS] + packed[2 * SLOTS : 3 * SLOTS]
        for slot in range(SLOTS):
            head = block * SLOTS + slot
            if head >= half_heads:
                continue
            lanes = slice(head * HEAD, (head + 1) * HEAD)
            base = slot * TEXT_ROWS
            pair = pay_ref[block, base : base + txt, :]
            folded = pay_ref[block, base + txt : base + TEXT_ROWS, :]
            tq_ref[:, lanes] = pair[:, :HEAD]
            tk_ref[:, lanes] = pair[:, HEAD:]
            tv_ref[:, lanes] = jnp.concatenate([folded[:, :HEAD], folded[:, HEAD:]], 0)
            tg_ref[:, lanes] = sums[slot : slot + 1, HEAD:]
            for dest in range(row_ref.shape[0]):
                row_ref[dest, :, lanes] = sums[slot : slot + 1, :HEAD]


def modulation_kernel(cond_ref, gate_ref, out_ref):
    cond = cond_ref[...]
    gates = jnp.concatenate(split_three(gate_ref[...]), 0)
    out_ref[...] = lax.dot_general(
        jnp.concatenate([cond, cond, cond], 0),
        gates,
        (((0,), (0,)), ((), ())),
        preferred_element_type=f32,
    )


def unpack_kernel(half_heads, chunks, *refs):
    back_refs, (q_ref, k_ref, v_ref) = refs[:-3], refs[-3:]
    rows = q_ref.shape[0]
    half = rows // 2
    pieces = {}
    for slots, back_ref in zip(chunks, back_refs):
        count = len(slots)
        for source in range(back_ref.shape[0]):
            for position, slot in enumerate(slots):
                head = head_of(source, slot, half_heads)
                if head is None:
                    continue
                begin = (count + position // 2) * rows
                if position % 2 == 1:
                    value = back_ref[source, begin : begin + rows, HEAD:]
                elif position < count - 1:
                    value = back_ref[source, begin : begin + rows, :HEAD]
                else:
                    folded = back_ref[source, begin : begin + half, :]
                    value = jnp.concatenate([folded[:, :HEAD], folded[:, HEAD:]], 0)
                pair = back_ref[source, position * rows : (position + 1) * rows, :]
                pieces[head] = (pair[:, :HEAD], pair[:, HEAD:], value)
    for head in range(0, 2 * half_heads, 2):
        lanes = slice(head * HEAD, (head + 2) * HEAD)
        for which, ref in enumerate((q_ref, k_ref, v_ref)):
            ref[:, lanes] = jnp.concatenate([pieces[head][which], pieces[head + 1][which]], 1)


def shards(
    img_query,
    img_key,
    img_value,
    img_cotangent,
    txt_query,
    txt_key,
    txt_value,
    txt_cotangent,
    img_gate,
    txt_gate,
    conditioning,
    norm_gains,
):
    _, rows, width = img_query.shape
    _, txt, half_width = txt_query.shape
    half_heads = half_width // HEAD
    blocks, halves, samples = lax.axis_size("blk"), lax.axis_size("uly"), lax.axis_size("dp")
    devices = blocks * halves
    chunks = (tuple(range(SLOTS)),)
    params = pltpu.CompilerParams(vmem_limit_bytes=VMEM)
    place = lax.axis_index("blk") * halves + lax.axis_index("uly")

    vmem = pl.BlockSpec(memory_space=pltpu.VMEM)
    packed = pl.pallas_call(
        functools.partial(pack_kernel, half_heads, chunks),
        in_specs=[pl.BlockSpec(memory_space=pltpu.SMEM)] + [vmem] * 10,
        out_specs=[vmem] * (len(chunks) + 2),
        out_shape=[
            jax.ShapeDtypeStruct((devices, 2 * len(slots) * rows, PAIR), bf16) for slots in chunks
        ]
        + [
            jax.ShapeDtypeStruct((txt, 2 * SLOTS * PAIR), bf16),
            jax.ShapeDtypeStruct((SLOTS, 2, PAIR), f32),
        ],
        compiler_params=params,
        name="pack",
    )(
        place[None],
        img_query[0],
        img_key[0],
        img_value[0],
        img_cotangent[0],
        txt_query[0],
        txt_key[0],
        txt_value[0],
        txt_cotangent[0],
        img_gate,
        txt_gate,
    )
    sends, text_rows, gates = packed[:-2], packed[-2], packed[-1]
    gains = norm_gains.reshape(2, PAIR)

    width_rows = width // blocks
    cond_rows = lax.dynamic_slice_in_dim(
        conditioning, lax.axis_index("blk") * width_rows, width_rows, 1
    )
    cond_all = lax.all_to_all(
        jnp.broadcast_to(cond_rows[None], (samples, 1, width_rows)), "dp", 0, 0, tiled=True
    ).reshape(samples, width_rows)

    received = [lax.all_to_all(send, ("blk", "uly"), 0, 0, tiled=True) for send in sends]
    backs = []
    for slots, arrived in zip(chunks, received):
        count = len(slots)
        out_rows = (2 * count + count) * rows // 2
        back, pay = pl.pallas_call(
            functools.partial(attend_kernel, count),
            grid=(count,),
            in_specs=[
                pl.BlockSpec((devices, 2 * rows, PAIR), lambda h: (0, h, 0)),
                pl.BlockSpec((txt, 2 * PAIR), lambda h: (0, h)),
                pl.BlockSpec((2, PAIR), lambda h: (0, 0)),
                pl.BlockSpec((1, 2, PAIR), lambda h: (h, 0, 0)),
            ],
            out_specs=[
                pl.BlockSpec((devices, out_rows, PAIR), lambda h: (0, 0, 0)),
                pl.BlockSpec((blocks, GATE_ROW + 16, PAIR), lambda h: (0, 0, 0)),
            ],
            out_shape=[
                jax.ShapeDtypeStruct((devices, out_rows, PAIR), bf16),
                jax.ShapeDtypeStruct((blocks, GATE_ROW + 16, PAIR), bf16),
            ],
            scratch_shapes=[pltpu.VMEM((8, PAIR), f32)],
            compiler_params=params,
            name="attend",
        )(arrived, text_rows, gains, gates)
        backs.append(lax.all_to_all(back, ("blk", "uly"), 0, 0, tiled=True))
    pays = lax.all_to_all(pay, "blk", 0, 0, tiled=True)

    tq_grad, tk_grad, tv_grad, txt_gate_grad, gate_rows = pl.pallas_call(
        functools.partial(text_kernel, half_heads),
        in_specs=[vmem],
        out_specs=[vmem] * 5,
        out_shape=[jax.ShapeDtypeStruct((txt, half_width), bf16)] * 3
        + [
            jax.ShapeDtypeStruct((1, half_width), f32),
            jax.ShapeDtypeStruct((samples, 1, half_width), f32),
        ],
        compiler_params=params,
        name="text",
    )(pays)
    gate_all = lax.all_to_all(gate_rows, "dp", 0, 0, tiled=True).reshape(samples, half_width)
    modulation_grad = pl.pallas_call(
        modulation_kernel,
        in_specs=[vmem] * 2,
        out_specs=vmem,
        out_shape=jax.ShapeDtypeStruct((width_rows, half_width), f32),
        compiler_params=params,
        name="modulation",
    )(cond_all, gate_all)
    out_query, out_key, out_value = pl.pallas_call(
        functools.partial(unpack_kernel, half_heads, chunks),
        in_specs=[vmem] * len(backs),
        out_specs=[vmem] * 3,
        out_shape=[jax.ShapeDtypeStruct((rows, width), bf16)] * 3,
        compiler_params=params,
        name="unpack",
    )(*backs)
    return (
        out_query[None],
        out_key[None],
        out_value[None],
        tq_grad[None],
        tk_grad[None],
        tv_grad[None],
        modulation_grad,
        txt_gate_grad,
    )


def solution(mesh):
    in_specs = (
        P("dp", ("blk", "uly"), None),
        P("dp", ("blk", "uly"), None),
        P("dp", ("blk", "uly"), None),
        P("dp", ("blk", "uly"), None),
        P("dp", None, "uly"),
        P("dp", None, "uly"),
        P("dp", None, "uly"),
        P("dp", None, "uly"),
        P("dp", None),
        P("dp", None),
        P("dp", None),
        P(),
    )
    out_specs = (
        P("dp", ("blk", "uly"), None),
        P("dp", ("blk", "uly"), None),
        P("dp", ("blk", "uly"), None),
        P("dp", None, "uly"),
        P("dp", None, "uly"),
        P("dp", None, "uly"),
        P("blk", "uly"),
        P("dp", "uly"),
    )
    return jax.shard_map(shards, mesh=mesh, in_specs=in_specs, out_specs=out_specs, check_vma=False)
```

profile of v0, /device:TPU:1, one launch (start us, length us, event | category | flops | bytes accessed | tf_op | source)
XLA Modules:
  0.0 170.0 jit_solution(15588356728756191414)
XLA Ops:
  0.7 4.1 %pack.1 = (bf16[8,1280,128]{2,1,0:T(8,128)(2,1)}, bf16[32,1280]{1,0:T(8,128)(2,1)}, f32[5,2,128]{2,1,0:T(2,128)}) custom-call(s32[1]{0:T(128)} %bitcast.place_ref, bf16[128,2432]{1,0:T(8,128)(2,1)} %bitcast.22, bf16[128,2432]{1,0:T(8,128)(2,1)} %bitcast.23, bf16[128,2432]{1,0:T(8,128)(2,1)} %bitcast.24, bf16[128,2432]{1,0:T(8,128)(2,1)} %bitcast.25, ...), custom_call_target="tpu_custom_call" | custom-call | tf_op jit(solution)/shard_map/pack/pallas_call | solution.py:313
  4.7 6.0 %all-to-all-start = ((bf16[8,1280,128]{2,1,0:T(8,128)(2,1)}), bf16[8,1280,128]{2,1,0:T(8,128)(2,1)S(1)}, u32[]{:S(2)}, u32[]{:S(2)}) async-start(bf16[8,1280,128]{2,1,0:T(8,128)(2,1)} %get-tuple-element.21), calls=%async_computation | async-start | bytes 5242880 | tf_op jit(solution)/shard_map/all_to_all | solution.py:350
  10.7 0.6 reshape.28.gain_ref
  11.4 37.1 %all-to-all-done.in_ref = bf16[8,1280,128]{2,1,0:T(8,128)(2,1)S(1)} async-done(((bf16[8,1280,128]{2,1,0:T(8,128)(2,1)}), bf16[8,1280,128]{2,1,0:T(8,128)(2,1)S(1)}, u32[]{:S(2)}, u32[]{:S(2)}) %all-to-all-start) | async-done | bytes 2621472 | tf_op jit(solution)/shard_map/all_to_all | solution.py:350
  48.5 1.5 copy-done.1
  50.0 36.4 %attend.1 = (bf16[8,960,128]{2,1,0:T(8,128)(2,1)}, bf16[4,256,128]{2,1,0:T(8,128)(2,1)}) custom-call(bf16[8,1280,128]{2,1,0:T(8,128)(2,1)} %copy-done.1, bf16[32,1280]{1,0:T(8,128)(2,1)} %get-tuple-element.22.text_ref, f32[2,128]{1,0:T(2,128)} %reshape.28.gain_ref, f32[5,2,128]{2,1,0:T(2,128)} %get-tuple-element.23.gate_ref), custom_call_target="tpu_custom_call" | custom-call | tf_op jit(solution)/shard_map/attend/pallas_call | solution.py:355
  86.4 3.4 %all-to-all-start.2 = ((bf16[4,256,128]{2,1,0:T(8,128)(2,1)}), bf16[4,256,128]{2,1,0:T(8,128)(2,1)S(1)}, u32[]{:S(2)}, u32[]{:S(2)}) async-start(bf16[4,256,128]{2,1,0:T(8,128)(2,1)} %get-tuple-element.28), calls=%async_computation.2 | async-start | bytes 524288 | tf_op jit(solution)/shard_map/all_to_all | solution.py:377
  89.8 0.1 dynamic-slice_reduce_fusion
  90.0 0.5 broadcast.2
  90.5 0.9 reduce.2
  91.4 0.7 reshape.32
  92.1 3.2 %all-to-all-done.2.pay_ref = bf16[4,256,128]{2,1,0:T(8,128)(2,1)S(1)} async-done(((bf16[4,256,128]{2,1,0:T(8,128)(2,1)}), bf16[4,256,128]{2,1,0:T(8,128)(2,1)S(1)}, u32[]{:S(2)}, u32[]{:S(2)}) %all-to-all-start.2) | async-done | bytes 262176 | tf_op jit(solution)/shard_map/all_to_all | solution.py:377
  95.3 13.7 %all-to-all-start.3 = ((bf16[32,2,304]{2,1,0:T(2,128)(2,1)}), bf16[32,2,304]{2,1,0:T(2,128)(2,1)S(1)}, u32[]{:S(2)}, u32[]{:S(2)}) async-start(bf16[32,2,304]{2,1,0:T(2,128)(2,1)} %reshape.32), calls=%async_computation.3 | async-start | bytes 98304 | tf_op jit(solution)/shard_map/all_to_all | solution.py:346
  109.1 2.1 %text.1 = (bf16[32,1216]{1,0:T(8,128)(2,1)}, bf16[32,1216]{1,0:T(8,128)(2,1)}, bf16[32,1216]{1,0:T(8,128)(2,1)}, f32[1,1216]{1,0:T(1,128)}, f32[32,1,1216]{2,1,0:T(1,128)}) custom-call(bf16[4,256,128]{2,1,0:T(8,128)(2,1)} %copy-done.3), custom_call_target="tpu_custom_call" | custom-call | tf_op jit(solution)/shard_map/text/pallas_call | solution.py:379
  111.1 7.3 %all-to-all-done.3 = bf16[32,2,304]{2,1,0:T(2,128)(2,1)S(1)} async-done(((bf16[32,2,304]{2,1,0:T(2,128)(2,1)}), bf16[32,2,304]{2,1,0:T(2,128)(2,1)S(1)}, u32[]{:S(2)}, u32[]{:S(2)}) %all-to-all-start.3) | async-done | bytes 38944 | tf_op jit(solution)/shard_map/all_to_all | solution.py:346
  118.5 15.8 %all_to_all.25 = f32[32,1,1216]{2,1,0:T(1,128)S(1)} all-to-all(f32[32,1,1216]{2,1,0:T(1,128)} %get-tuple-element.32), channel_id=1, replica_groups=mesh['dp'=32,'blk'=4,'uly'=2] {'dp'}, dimensions={0} | all-to-all | bytes 311296 | tf_op jit(solution)/shard_map/all_to_all | solution.py:391
  134.3 3.6 %all-to-all-start.1 = ((bf16[8,960,128]{2,1,0:T(8,128)(2,1)}), bf16[8,960,128]{2,1,0:T(8,128)(2,1)S(1)}, u32[]{:S(2)}, u32[]{:S(2)}) async-start(bf16[8,960,128]{2,1,0:T(8,128)(2,1)} %get-tuple-element.24), calls=%async_computation.1 | async-start | bytes 3932160 | tf_op jit(solution)/shard_map/all_to_all | solution.py:376
  137.9 0.1 reshape.33
  138.0 0.6 copy.26
  138.6 0.7 copy.25
  139.3 3.2 %modulation.1 = f32[608,1216]{1,0:T(8,128)} custom-call(bf16[32,608]{1,0:T(8,128)(2,1)} %bitcast.26, f32[32,1216]{1,0:T(8,128)} %bitcast.21), custom_call_target="tpu_custom_call" | custom-call | tf_op jit(solution)/shard_map/modulation/pallas_call | solution.py:392
  142.5 22.9 %all-to-all-done.1.refs_0_ = bf16[8,960,128]{2,1,0:T(8,128)(2,1)S(1)} async-done(((bf16[8,960,128]{2,1,0:T(8,128)(2,1)}), bf16[8,960,128]{2,1,0:T(8,128)(2,1)S(1)}, u32[]{:S(2)}, u32[]{:S(2)}) %all-to-all-start.1) | async-done | bytes 1966112 | tf_op jit(solution)/shard_map/all_to_all | solution.py:376
  165.4 1.3 copy-done.2
  166.7 3.3 %unpack.1 = (bf16[128,2432]{1,0:T(8,128)(2,1)}, bf16[128,2432]{1,0:T(8,128)(2,1)}, bf16[128,2432]{1,0:T(8,128)(2,1)}) custom-call(bf16[8,960,128]{2,1,0:T(8,128)(2,1)} %copy-done.2), custom_call_target="tpu_custom_call" | custom-call | tf_op jit(solution)/shard_map/unpack/pallas_call | solution.py:400
  (9 shorter events, 0.1 us)
Async XLA Ops:
  0.6 89.2 %copy-start = (bf16[1,2432]{1,0:T(2,128)(2,1)S(1)}, bf16[1,2432]{1,0:T(2,128)(2,1)}, u32[]{:S(2)}) copy-start(bf16[1,2432]{1,0:T(2,128)(2,1)} %param.22) | copy-start | bytes 14596
  4.7 6.0 %copy-start.4 = (f32[4,64]{1,0:T(4,128)S(1)}, f32[4,64]{1,0:T(4,128)}, u32[]{:S(2)}) copy-start(f32[4,64]{1,0:T(4,128)} %param.23) | copy-start | bytes 3076
  4.7 43.8 %all-to-all-start = ((bf16[8,1280,128]{2,1,0:T(8,128)(2,1)}), bf16[8,1280,128]{2,1,0:T(8,128)(2,1)S(1)}, u32[]{:S(2)}, u32[]{:S(2)}) async-start(bf16[8,1280,128]{2,1,0:T(8,128)(2,1)} %get-tuple-element.21), calls=%async_computation | async-start | bytes 5242880 | tf_op jit(solution)/shard_map/all_to_all | solution.py:350
  48.5 1.5 copy-start.1
  86.4 8.9 %all-to-all-start.2 = ((bf16[4,256,128]{2,1,0:T(8,128)(2,1)}), bf16[4,256,128]{2,1,0:T(8,128)(2,1)S(1)}, u32[]{:S(2)}, u32[]{:S(2)}) async-start(bf16[4,256,128]{2,1,0:T(8,128)(2,1)} %get-tuple-element.28), calls=%async_computation.2 | async-start | bytes 524288 | tf_op jit(solution)/shard_map/all_to_all | solution.py:377
  95.3 13.8 %copy-start.3 = (bf16[4,256,128]{2,1,0:T(8,128)(2,1)}, bf16[4,256,128]{2,1,0:T(8,128)(2,1)S(1)}, u32[]{:S(2)}) copy-start(bf16[4,256,128]{2,1,0:T(8,128)(2,1)S(1)} %all-to-all-done.2.pay_ref) | copy-start | bytes 786436
  95.3 23.2 %all-to-all-start.3 = ((bf16[32,2,304]{2,1,0:T(2,128)(2,1)}), bf16[32,2,304]{2,1,0:T(2,128)(2,1)S(1)}, u32[]{:S(2)}, u32[]{:S(2)}) async-start(bf16[32,2,304]{2,1,0:T(2,128)(2,1)} %reshape.32), calls=%async_computation.3 | async-start | bytes 98304 | tf_op jit(solution)/shard_map/all_to_all | solution.py:346
  134.3 31.2 %all-to-all-start.1 = ((bf16[8,960,128]{2,1,0:T(8,128)(2,1)}), bf16[8,960,128]{2,1,0:T(8,128)(2,1)S(1)}, u32[]{:S(2)}, u32[]{:S(2)}) async-start(bf16[8,960,128]{2,1,0:T(8,128)(2,1)} %get-tuple-element.24), calls=%async_computation.1 | async-start | bytes 3932160 | tf_op jit(solution)/shard_map/all_to_all | solution.py:376
  165.4 1.3 copy-start.2
where the time goes:
time: 171 us; the launch traced here: 170 us
  waiting for transfers between devices  70.6 us (41%)
  Pallas kernels  49 us (29%)
  starting transfers between devices  26.7 us (16%)
  blocking collectives  15.8 us (9%)
  local copies, waits for them, and re-layouts  6.26 us (4%)
    all_to_all x1, waiting for transfers between devices, shards(): lax.all_to_all(send, ('blk', 'uly'), 0, 0, tiled=True)  37.1 us
    pallas_call x1, Pallas kernels, shards(): pl.pallas_call(functools.partial(attend_kernel, count), grid=(count,), in...  36.4 us
    all_to_all x1, waiting for transfers between devices, shards(): backs.append(lax.all_to_all(back, ('blk', 'uly'), 0, 0, tiled=True))  22.9 us
    all_to_all x1, blocking collectives, shards(): lax.all_to_all(gate_rows, 'dp', 0, 0, tiled=True)  15.8 us
    all_to_all x1, starting transfers between devices, shards(): lax.all_to_all(jnp.broadcast_to(cond_rows[None], (samples, 1, width_rows)...  13.7 us
    all_to_all x1, waiting for transfers between devices, shards(): lax.all_to_all(jnp.broadcast_to(cond_rows[None], (samples, 1, width_rows)...  7.31 us
    all_to_all x1, starting transfers between devices, shards(): lax.all_to_all(send, ('blk', 'uly'), 0, 0, tiled=True)  6 us
    unnamed x14, local copies, waits for them, and re-layouts  4.96 us
  transfers between devices with their start and end apart: 4, of which 4 were waited for; matrix products, arithmetic and copies ran while one was open for 3% of the time, Pallas kernels for 3%

commit v1 on v0

v1 whole, which is shorter than its diff:
```python
import functools

import jax
import jax.numpy as jnp
from jax import lax
from jax.experimental import pallas as pl
from jax.experimental.pallas import tpu as pltpu
from jax.sharding import PartitionSpec as P

HEAD = 64
PAIR = 2 * HEAD
EPS = 1e-06
SLOTS = 5
TEXT_ROWS = 48
GATE_ROWS = 16
ROUTES = 8
CHUNKS = ((0, 1, 2), (3, 4))
VMEM = 56 * 2**20
f32 = jnp.float32
bf16 = jnp.bfloat16


def head_of(dest, slot, half_heads):
    place = (dest // 2) * SLOTS + slot
    return (dest % 2) * half_heads + place if place < half_heads else None


def matmul(left, right):
    return jnp.dot(left, right, preferred_element_type=f32)


def matmul_nt(left, right):
    return lax.dot_general(left, right, (((1,), (1,)), ((), ())), preferred_element_type=f32)


def split_two(wide):
    high = wide.astype(bf16)
    return high, (wide - high.astype(f32)).astype(bf16)


def split_three(wide):
    high = wide.astype(bf16)
    rest = wide - high.astype(f32)
    middle = rest.astype(bf16)
    return high, middle, (rest - middle.astype(f32)).astype(bf16)


def half_means(wide, averager):
    return matmul(jnp.concatenate(split_two(wide), 1), averager)


def route(place, index, way=1):
    blocks = ROUTES // 2
    return ((place // 2 + blocks + way * (index // 2)) % blocks) * 2 + (place + index) % 2


def pack_kernel(
    half_heads,
    chunks,
    place_ref,
    iq_ref,
    ik_ref,
    iv_ref,
    ic_ref,
    tq_ref,
    tk_ref,
    tv_ref,
    tc_ref,
    ig_ref,
    tg_ref,
    *out_refs,
):
    send_refs, kept_refs = out_refs[: len(chunks)], out_refs[len(chunks) :]

    def columns(ref, head):
        return ref[:, head * HEAD : (head + 1) * HEAD]

    rows = iq_ref.shape[0]
    for slots, send_ref in zip(chunks, send_refs):
        for dest in range(send_ref.shape[0]):
            for position, slot in enumerate(slots):
                head = head_of(dest, slot, half_heads)
                for pair, (first, second) in enumerate(((iq_ref, ik_ref), (iv_ref, ic_ref))):
                    tile = (
                        jnp.zeros((rows, PAIR), bf16)
                        if head is None
                        else jnp.concatenate([columns(first, head), columns(second, head)], 1)
                    )
                    start = (2 * position + pair) * rows
                    send_ref[dest, start : start + rows, :] = tile
    if not kept_refs:
        return
    text_ref, gate_ref = kept_refs
    place = place_ref[0]
    for device in range(send_refs[0].shape[0]):

        @pl.when(place == device)
        def _():
            for slot in range(SLOTS):
                head = head_of(device, slot, half_heads)
                local = None if head is None else head - (device % 2) * half_heads
                for pair, (first, second) in enumerate(((tq_ref, tk_ref), (tv_ref, tc_ref))):
                    tile = (
                        jnp.zeros((first.shape[0], PAIR), bf16)
                        if local is None
                        else jnp.concatenate([columns(first, local), columns(second, local)], 1)
                    )
                    text_ref[:, (2 * slot + pair) * PAIR : (2 * slot + pair + 1) * PAIR] = tile
                for row, ref in enumerate((ig_ref, tg_ref)):
                    gate = jnp.zeros((1, HEAD), bf16) if head is None else columns(ref, head)
                    gate = gate.astype(f32)
                    gate_ref[slot, row : row + 1, :] = jnp.concatenate([gate, gate], 1)


def attend_kernel(slots, *refs):
    first, last = slots[0] == 0, slots[-1] == SLOTS - 1
    count = len(slots)
    in_ref, text_ref, gain_ref, gate_ref, *refs = refs
    if not first:
        place_ref, earlier_pay_ref, earlier_sum_ref, *refs = refs
    if first:
        out_ref, pay_ref, sum_ref = refs
    else:
        out_refs = refs
    devices, tile_rows = in_ref.shape[0], in_ref.shape[1] // (2 * count)
    rows, txt = devices * tile_rows, text_ref.shape[0]
    total_rows = rows + txt
    row_at = lax.broadcasted_iota(jnp.int32, (2 * PAIR, PAIR), 0)
    lane_at = lax.broadcasted_iota(jnp.int32, (2 * PAIR, PAIR), 1)
    averager = jnp.where((row_at % PAIR) // HEAD == lane_at // HEAD, 1.0 / HEAD, 0.0).astype(bf16)
    ones = jnp.ones((2 * PAIR, PAIR), bf16)
    lane = lax.broadcasted_iota(jnp.int32, (total_rows, PAIR), 1)
    gain = jnp.concatenate(
        [
            jnp.broadcast_to(gain_ref[0:1, :], (rows, PAIR)),
            jnp.broadcast_to(gain_ref[1:2, :], (txt, PAIR)),
        ],
        0,
    )
    heads = range(count)

    def joint(head, pair):
        tile = 2 * head + pair
        at = slice(tile * tile_rows, (tile + 1) * tile_rows)
        if first:
            image = in_ref[:, at, :].reshape(rows, PAIR)
        else:
            order = [route(place_ref[0], index, -1) for index in range(devices)]
            image = jnp.concatenate([in_ref[device, at, :] for device in order], 0)
        place = 2 * slots[head] + pair
        return jnp.concatenate([image, text_ref[:, place * PAIR : (place + 1) * PAIR]], 0)

    raw = [joint(head, 0).astype(f32) for head in heads]
    value_cotan = [joint(head, 1) for head in heads]
    inverse = [lax.rsqrt(half_means(x * x, averager) + EPS) for x in raw]
    normed = [(x * inv * gain).astype(bf16) for x, inv in zip(raw, inverse)]
    queries = [x[:, :HEAD] for x in normed]
    keys = [x[:, HEAD:] for x in normed]
    blank = jnp.zeros((total_rows, HEAD), bf16)
    values_ones = [
        jnp.concatenate([x[:, :HEAD], jnp.ones((total_rows, HEAD), bf16)], 1) for x in value_cotan
    ]
    keys_zeros = [jnp.concatenate([x, blank], 1) for x in keys]
    cotan = [x[:, HEAD:].astype(f32) for x in value_cotan]

    def upstream_of(head):
        slot = slots[head]
        gate = jnp.concatenate(
            [
                jnp.broadcast_to(gate_ref[slot, 0:1, :HEAD], (rows, HEAD)),
                jnp.broadcast_to(gate_ref[slot, 1:2, :HEAD], (txt, HEAD)),
            ],
            0,
        )
        return (cotan[head] * gate).astype(bf16).astype(f32)

    upstream = [upstream_of(head) for head in heads]
    scores = [matmul_nt(q * jnp.asarray(0.125, bf16), k) for q, k in zip(queries, keys)]
    exponent = [jnp.exp(x).astype(bf16) for x in scores]
    weighted = [matmul(e, v) for e, v in zip(exponent, values_ones)]

    def scaled_upstream(head):
        over_total = 1.0 / weighted[head][:, HEAD:]
        attention = (weighted[head][:, :HEAD] * over_total).astype(bf16).astype(f32)
        scaled = (upstream[head] * over_total).astype(bf16)
        product = jnp.concatenate([scaled.astype(f32) * attention, blank.astype(f32)], 1)
        delta = matmul(jnp.concatenate(split_two(product), 1), ones)
        delta_high, delta_low = split_two(delta)
        extended = jnp.where(
            lane < HEAD,
            jnp.concatenate([scaled, blank], 1),
            jnp.where(
                lane == HEAD,
                -delta_high,
                jnp.where(lane == HEAD + 1, -delta_low, jnp.zeros_like(delta_low)),
            ),
        )
        gated = cotan[head] * attention
        sums = jnp.concatenate(
            [
                jnp.sum(gated[:rows], 0, keepdims=True),
                jnp.sum(gated[rows:], 0, keepdims=True),
            ],
            1,
        )
        return scaled, extended, sums

    prepared = [scaled_upstream(head) for head in heads]
    value_grad_t = [matmul(x[0].T, e) for x, e in zip(prepared, exponent)]
    prob_grad = [matmul_nt(x[1], v) for x, v in zip(prepared, values_ones)]
    score_grad = [e * x.astype(bf16) for e, x in zip(exponent, prob_grad)]
    query_grad = [matmul(x, k) for x, k in zip(score_grad, keys_zeros)]
    value_key_grad = [
        jnp.concatenate([v, matmul(q.T, x)], 0).T
        for v, q, x in zip(value_grad_t, queries, score_grad)
    ]

    half = tile_rows // 2
    text_tiles = []
    for head in heads:
        scaled = jnp.where(lane < HEAD, query_grad[head], value_key_grad[head]) * (gain * 0.125)
        mean = half_means(raw[head] * scaled, averager)
        inv = inverse[head]
        pair_grad = (inv * scaled - raw[head] * (inv * inv * inv) * mean).astype(bf16)
        value_grad = value_key_grad[head][:, :HEAD].astype(bf16)
        begin = (count + head // 2) * tile_rows
        pairs = pair_grad[:rows].reshape(devices, tile_rows, PAIR)
        tiles = value_grad[:rows].reshape(devices, tile_rows, HEAD)
        targets = [(out_ref, slice(None))] if first else [(r, i) for i, r in enumerate(out_refs)]
        for ref, device in targets:
            value = tiles[device]
            ref[..., head * tile_rows : (head + 1) * tile_rows, :] = pairs[device]
            if head % 2 == 1:
                ref[..., begin : begin + tile_rows, HEAD:] = value
            elif head < count - 1:
                ref[..., begin : begin + tile_rows, :HEAD] = value
            else:
                ref[..., begin : begin + half, :] = jnp.concatenate(
                    [value[..., :half, :], value[..., half:, :]], -1
                )
        text_grad = value_grad[rows:]
        text_tiles += [
            pair_grad[rows:],
            jnp.concatenate([text_grad[: txt // 2], text_grad[txt // 2 :]], 1),
        ]
    sums = [x[2] for x in prepared]
    if not first:
        sums = [earlier_sum_ref[slot : slot + 1, :] for slot in range(slots[0])] + sums
    if not last:
        pay_ref[...] = jnp.concatenate(text_tiles, 0)
        sum_ref[...] = jnp.concatenate(sums + [jnp.zeros((8 - len(sums), PAIR), f32)], 0)
        return
    packed = [part.astype(f32) for part in split_three(jnp.concatenate(sums, 0))]
    packed = jnp.concatenate(packed + [jnp.zeros((GATE_ROWS - 3 * SLOTS, PAIR), f32)], 0)
    pay = jnp.concatenate([earlier_pay_ref[...]] + text_tiles + [packed.astype(bf16)], 0)
    for ref in out_refs[::2]:
        ref[ref.shape[0] - pay.shape[0] :, :] = pay


def pay_of(ref):
    start = ref.shape[0] - SLOTS * TEXT_ROWS - GATE_ROWS
    packed = ref[start + SLOTS * TEXT_ROWS :, :].astype(f32)
    return start, packed[:SLOTS] + packed[SLOTS : 2 * SLOTS] + packed[2 * SLOTS : 3 * SLOTS]


def spread_kernel(half_heads, place_ref, cond_ref, *refs):
    pay_refs, out_ref = refs[:-1], refs[-1]
    blocks = len(pay_refs)
    cond = cond_ref[...].astype(f32)
    for place in range(blocks):

        @pl.when(place_ref[0] // 2 == place)
        def _():
            heads = []
            for block in range(blocks):
                used = min(SLOTS, half_heads - block * SLOTS)
                sums = pay_of(pay_refs[(block - place) % blocks])[1]
                heads += [sums[slot : slot + 1, :HEAD] for slot in range(used)]
            rows = []
            for row in (jnp.concatenate(heads, 1), cond):
                spare = jnp.zeros((1, -row.shape[1] % PAIR), f32)
                row = jnp.concatenate([row, spare], 1)
                rows += [row[:, at : at + PAIR] for at in range(0, row.shape[1], PAIR)]
            rows.append(jnp.zeros((out_ref.shape[1] - len(rows), PAIR), f32))
            tile = jnp.concatenate(rows, 0).astype(bf16)
            for dest in range(out_ref.shape[0]):
                out_ref[dest] = tile


def modulation_kernel(in_ref, out_ref, wide_ref):
    samples, tile_rows, _ = in_ref.shape
    rows, width = out_ref.shape
    wide_ref[...] = in_ref[...].astype(f32).reshape(samples * tile_rows, PAIR)

    def over_samples(start, count):
        parts = [
            wide_ref[pl.ds(start + row, samples, stride=tile_rows), :]
            for row in range(pl.cdiv(count, PAIR))
        ]
        return jnp.concatenate(parts, 1)[:, :count].astype(bf16)

    out_ref[...] = lax.dot_general(
        over_samples(pl.cdiv(width, PAIR), rows),
        over_samples(0, width),
        (((0,), (0,)), ((), ())),
        preferred_element_type=f32,
    )


def unpack_kernel(half_heads, chunks, place_ref, first_ref, *refs):
    routed_refs, outs = refs[:ROUTES], refs[ROUTES:]
    q_ref, k_ref, v_ref, tq_ref, tk_ref, tv_ref, tg_ref, held_ref = outs
    for index, ref in enumerate(routed_refs):
        held_ref[route(place_ref[0], index)] = ref[: held_ref.shape[1], :]
    back_refs = (first_ref, held_ref)
    rows = q_ref.shape[0]
    half = rows // 2
    pieces = {}
    for slots, back_ref in zip(chunks, back_refs):
        count = len(slots)
        for source in range(back_ref.shape[0]):
            for position, slot in enumerate(slots):
                head = head_of(source, slot, half_heads)
                if head is None:
                    continue
                begin = (count + position // 2) * rows
                if position % 2 == 1:
                    value = back_ref[source, begin : begin + rows, HEAD:]
                elif position < count - 1:
                    value = back_ref[source, begin : begin + rows, :HEAD]
                else:
                    folded = back_ref[source, begin : begin + half, :]
                    value = jnp.concatenate([folded[:, :HEAD], folded[:, HEAD:]], 0)
                pair = back_ref[source, position * rows : (position + 1) * rows, :]
                pieces[head] = (pair[:, :HEAD], pair[:, HEAD:], value)
    for head in range(0, 2 * half_heads, 2):
        lanes = slice(head * HEAD, (head + 2) * HEAD)
        for which, ref in enumerate((q_ref, k_ref, v_ref)):
            ref[:, lanes] = jnp.concatenate([pieces[head][which], pieces[head + 1][which]], 1)

    txt = tq_ref.shape[0]
    pay_refs = routed_refs[::2]

    def place_text(block, pay_ref):
        start, sums = pay_of(pay_ref)
        for slot in range(min(SLOTS, half_heads - block * SLOTS)):
            head = block * SLOTS + slot
            lanes = slice(head * HEAD, (head + 1) * HEAD)
            base = start + slot * TEXT_ROWS
            pair = pay_ref[base : base + txt, :]
            folded = pay_ref[base + txt : base + TEXT_ROWS, :]
            tq_ref[:, lanes] = pair[:, :HEAD]
            tk_ref[:, lanes] = pair[:, HEAD:]
            tv_ref[:, lanes] = jnp.concatenate([folded[:, :HEAD], folded[:, HEAD:]], 0)
            tg_ref[:, lanes] = sums[slot : slot + 1, HEAD:]

    blocks = len(pay_refs)
    for shift in range(blocks):
        for block in range(blocks):

            @pl.when(place_ref[0] // 2 == (block - shift) % blocks)
            def _():
                place_text(block, pay_refs[shift])


def shards(
    img_query,
    img_key,
    img_value,
    img_cotangent,
    txt_query,
    txt_key,
    txt_value,
    txt_cotangent,
    img_gate,
    txt_gate,
    conditioning,
    norm_gains,
):
    _, rows, width = img_query.shape
    _, txt, half_width = txt_query.shape
    half_heads = half_width // HEAD
    blocks, halves, samples = lax.axis_size("blk"), lax.axis_size("uly"), lax.axis_size("dp")
    devices = blocks * halves
    params = pltpu.CompilerParams(vmem_limit_bytes=VMEM)
    place = lax.axis_index("blk") * halves + lax.axis_index("uly")
    vmem = pl.BlockSpec(memory_space=pltpu.VMEM)
    shape = jax.ShapeDtypeStruct

    def call(kernel, outs, operands, name, cost=None, smem=0, scratch=()):
        return pl.pallas_call(
            kernel,
            in_specs=[pl.BlockSpec(memory_space=pltpu.SMEM)] * smem + [vmem] * (len(operands) - smem),
            out_specs=[vmem] * len(outs),
            out_shape=outs,
            scratch_shapes=scratch,
            compiler_params=params,
            cost_estimate=cost,
            name=name,
        )(*operands)

    def exchange(operand, axes):
        return lax.all_to_all(operand, axes, 0, 0, tiled=True)

    image = (img_query[0], img_key[0], img_value[0], img_cotangent[0])
    text = (txt_query[0], txt_key[0], txt_value[0], txt_cotangent[0])
    operands = (place[None], *image, *text, img_gate, txt_gate)
    sends = []
    kept = None
    for slots in CHUNKS:
        outs = [shape((devices, 2 * len(slots) * rows, PAIR), bf16)]
        if kept is None:
            outs += [
                shape((txt, 2 * SLOTS * PAIR), bf16),
                shape((SLOTS, 2, PAIR), f32),
            ]
        send, *others = call(
            functools.partial(pack_kernel, half_heads, (slots,)), outs, operands, "pack", smem=1
        )
        sends.append(send)
        if kept is None:
            kept = others
    text_rows, gates = kept
    gains = norm_gains.reshape(2, PAIR)

    width_rows = width // blocks
    cond_row = lax.dynamic_slice_in_dim(
        conditioning, lax.axis_index("blk") * width_rows, width_rows, 1
    )

    received = []
    for send in sends:
        if received:
            send, received[-1] = lax.optimization_barrier((send, received[-1]))
        received.append(exchange(send, ("blk", "uly")))
    earlier = ()
    total_rows = devices * rows + txt
    for slots, arrived in zip(CHUNKS, received):
        count = len(slots)
        last = slots[-1] == SLOTS - 1
        pay_rows = (slots[-1] + 1) * TEXT_ROWS + (GATE_ROWS if last else 0)
        outs = [
            shape((devices, 3 * count * rows // 2, PAIR), bf16),
            shape((pay_rows, PAIR), bf16),
            shape((8, PAIR), f32),
        ]
        if last:
            outs = [
                shape((3 * count * rows // 2 + (0 if index % 2 else pay_rows), PAIR), bf16)
                for index in range(ROUTES)
            ]
        cost = pl.CostEstimate(
            flops=count * 12 * total_rows * total_rows * HEAD * 4,
            bytes_accessed=count * devices * rows * HEAD * 14,
            transcendentals=count * total_rows * total_rows,
        )
        back = call(
            functools.partial(attend_kernel, slots),
            outs,
            (arrived, text_rows, gains, gates, *earlier),
            "attend",
            cost,
        )
        if not last:
            earlier = (place[None], *back[1:])
            back_first = exchange(back[0], ("blk", "uly"))
    back_first, *back = lax.optimization_barrier((back_first, *back))
    routed = [back[0]]
    for index in range(1, ROUTES):
        pairs = [(device, route(device, index, -1)) for device in range(devices)]
        routed.append(lax.ppermute(back[index], ("blk", "uly"), pairs))
    routed = lax.optimization_barrier(routed)
    tile_rows = -(-(pl.cdiv(half_width, PAIR) + pl.cdiv(width_rows, PAIR)) // 16) * 16
    (gate_rows,) = call(
        functools.partial(spread_kernel, half_heads),
        [shape((samples, tile_rows, PAIR), bf16)],
        (place[None], cond_row, *routed[::2]),
        "spread",
        smem=1,
    )
    (modulation_grad,) = call(
        modulation_kernel,
        [shape((width_rows, half_width), f32)],
        (exchange(gate_rows, "dp"),),
        "modulation",
        scratch=[pltpu.VMEM((samples * tile_rows, PAIR), f32)],
    )
    out_query, out_key, out_value, tq_grad, tk_grad, tv_grad, txt_gate_grad = call(
        functools.partial(unpack_kernel, half_heads, CHUNKS),
        [shape((rows, width), bf16)] * 3
        + [shape((txt, half_width), bf16)] * 3
        + [shape((1, half_width), f32)],
        (place[None], back_first, *routed),
        "unpack",
        smem=1,
        scratch=[pltpu.VMEM((devices, 3 * len(CHUNKS[1]) * rows // 2, PAIR), bf16)],
    )
    return (
        out_query[None],
        out_key[None],
        out_value[None],
        tq_grad[None],
        tk_grad[None],
        tv_grad[None],
        modulation_grad,
        txt_gate_grad,
    )


def solution(mesh):
    in_specs = (
        P("dp", ("blk", "uly"), None),
        P("dp", ("blk", "uly"), None),
        P("dp", ("blk", "uly"), None),
        P("dp", ("blk", "uly"), None),
        P("dp", None, "uly"),
        P("dp", None, "uly"),
        P("dp", None, "uly"),
        P("dp", None, "uly"),
        P("dp", None),
        P("dp", None),
        P("dp", None),
        P(),
    )
    out_specs = (
        P("dp", ("blk", "uly"), None),
        P("dp", ("blk", "uly"), None),
        P("dp", ("blk", "uly"), None),
        P("dp", None, "uly"),
        P("dp", None, "uly"),
        P("dp", None, "uly"),
        P("blk", "uly"),
        P("dp", "uly"),
    )
    return jax.shard_map(shards, mesh=mesh, in_specs=in_specs, out_specs=out_specs, check_vma=False)
```

time: 171 us -> 122 us (0.71)
  waiting for transfers between devices: 70.6 us -> 38.4 us
  blocking collectives: 15.8 us -> 0 us
  starting transfers between devices: 26.7 us -> 37.1 us
  Pallas kernels: 49 us -> 41.7 us
  local copies, waits for them, and re-layouts: 6.26 us -> 3.4 us
    all_to_all x4, waiting for transfers between devices: 70.6 us -> 30.7 us  [exchange(): return lax.all_to_all(operand, axes, 0, 0, tiled=True)]
    all_to_all x1 -> x0, blocking collectives: 15.8 us -> none  [shards(): lax.all_to_all(gate_rows, 'dp', 0, 0, tiled=True)]
    ppermute x0 -> x7, starting transfers between devices: none -> 8.3 us  [shards(): routed.append(lax.ppermute(back[index], ('blk', 'uly'), pairs))]
    ppermute x0 -> x7, waiting for transfers between devices: none -> 7.7 us  [shards(): routed.append(lax.ppermute(back[index], ('blk', 'uly'), pairs))]
    pallas_call x5 -> x7, Pallas kernels: 49 us -> 41.7 us  [call(): pl.pallas_call(kernel, in_specs=[pl.BlockSpec(memory_space=pltpu.SMEM)] *...]
    unnamed x14 -> x26, local copies, waits for them, and re-layouts: 4.96 us -> 2.09 us
    all_to_all x4, starting transfers between devices: 26.7 us -> 28.8 us  [exchange(): return lax.all_to_all(operand, axes, 0, 0, tiled=True)]
  transfers between devices with their start and end apart: 4 -> 11, of which waited for: 4 -> 6; matrix products, arithmetic and copies ran while one was open for 3% -> 1% of each run, Pallas kernels for 3% -> 27%
where the time goes in v1:
time: 122 us; the launch traced here: 121 us
  Pallas kernels  41.7 us (34%)
  waiting for transfers between devices  38.4 us (31%)
  starting transfers between devices  37.1 us (30%)
  local copies, waits for them, and re-layouts  3.4 us (3%)
    pallas_call x7, Pallas kernels, call(): pl.pallas_call(kernel, in_specs=[pl.BlockSpec(memory_space=pltpu.SMEM)] *...  41.7 us
    all_to_all x4, waiting for transfers between devices, exchange(): return lax.all_to_all(operand, axes, 0, 0, tiled=True)  30.7 us
    all_to_all x4, starting transfers between devices, exchange(): return lax.all_to_all(operand, axes, 0, 0, tiled=True)  28.8 us
    ppermute x7, starting transfers between devices, shards(): routed.append(lax.ppermute(back[index], ('blk', 'uly'), pairs))  8.3 us
    ppermute x7, waiting for transfers between devices, shards(): routed.append(lax.ppermute(back[index], ('blk', 'uly'), pairs))  7.7 us
  transfers between devices with their start and end apart: 11, of which 6 were waited for; matrix products, arithmetic and copies ran while one was open for 1% of the time, Pallas kernels for 27%

profile of v1, /device:TPU:1, one launch (start us, length us, event | category | flops | bytes accessed | tf_op | source)
XLA Modules:
  0.0 121.4 jit_solution(11569012676998189706)
XLA Ops:
  0.7 3.5 %pack.3 = (bf16[8,768,128]{2,1,0:T(8,128)(2,1)}, bf16[32,1280]{1,0:T(8,128)(2,1)}, f32[5,2,128]{2,1,0:T(2,128)}) custom-call(s32[1]{0:T(128)} %bitcast.place_ref.refs_4_, bf16[128,2432]{1,0:T(8,128)(2,1)} %bitcast.15, bf16[128,2432]{1,0:T(8,128)(2,1)} %bitcast.17, bf16[128,2432]{1,0:T(8,128)(2,1)} %bitcast.19, bf16[128,2432]{1,0:T(8,128)(2,1)} %bitcast.21, ...), custom_call_target="tpu_custom_call" | custom-call | tf_op jit(solution)/shard_map/pack/pallas_call | solution.py:391
  4.1 5.9 %all-to-all-start = ((bf16[8,768,128]{2,1,0:T(8,128)(2,1)}), bf16[8,768,128]{2,1,0:T(8,128)(2,1)S(1)}, u32[]{:S(2)}, u32[]{:S(2)}) async-start(bf16[8,768,128]{2,1,0:T(8,128)(2,1)} %get-tuple-element.48), calls=%async_computation | async-start | bytes 3145728 | tf_op jit(solution)/shard_map/all_to_all | solution.py:403
  10.0 3.0 %pack.2 = bf16[8,512,128]{2,1,0:T(8,128)(2,1)} custom-call(s32[1]{0:T(128)} %bitcast.place_ref.refs_4_, bf16[128,2432]{1,0:T(8,128)(2,1)} %bitcast.16, bf16[128,2432]{1,0:T(8,128)(2,1)} %bitcast.18, bf16[128,2432]{1,0:T(8,128)(2,1)} %bitcast.20, bf16[128,2432]{1,0:T(8,128)(2,1)} %bitcast.22, bf16[32,1216]{1,0:T(8,128)(2,1)} %bitcast.24, ...), custom_call_target="tpu_custom_call" | custom-call | tf_op jit(solution)/shard_map/pack/pallas_call | solution.py:391
  13.0 0.7 reshape.19.refs_2_
  13.7 19.4 %all-to-all-done.refs_0_ = bf16[8,768,128]{2,1,0:T(8,128)(2,1)S(1)} async-done(((bf16[8,768,128]{2,1,0:T(8,128)(2,1)}), bf16[8,768,128]{2,1,0:T(8,128)(2,1)S(1)}, u32[]{:S(2)}, u32[]{:S(2)}) %all-to-all-start) | async-done | bytes 1572896 | tf_op jit(solution)/shard_map/all_to_all | solution.py:403
  33.1 3.6 %all-to-all-start.2 = ((bf16[8,512,128]{2,1,0:T(8,128)(2,1)}), bf16[8,512,128]{2,1,0:T(8,128)(2,1)S(1)}, u32[]{:S(2)}, u32[]{:S(2)}) async-start(bf16[8,512,128]{2,1,0:T(8,128)(2,1)} %pack.2), calls=%async_computation.2 | async-start | bytes 2097152 | tf_op jit(solution)/shard_map/all_to_all | solution.py:403
  36.6 15.3 %attend.2 = (bf16[8,576,128]{2,1,0:T(8,128)(2,1)}, bf16[144,128]{1,0:T(8,128)(2,1)}, f32[8,128]{1,0:T(8,128)}) custom-call(bf16[8,768,128]{2,1,0:T(8,128)(2,1)} %copy-done.2, bf16[32,1280]{1,0:T(8,128)(2,1)} %get-tuple-element.50.refs_1_, f32[2,128]{1,0:T(2,128)} %reshape.19.refs_2_, f32[5,2,128]{2,1,0:T(2,128)} %get-tuple-element.51.refs_3_), custom_call_target="tpu_custom_call" | custom-call | flops 10277093376 | bytes 2752512 | tf_op jit(solution)/shard_map/attend/pallas_call | solution.py:391
  51.9 5.1 %all-to-all-start.1 = ((bf16[8,576,128]{2,1,0:T(8,128)(2,1)}), bf16[8,576,128]{2,1,0:T(8,128)(2,1)S(1)}, u32[]{:S(2)}, u32[]{:S(2)}) async-start(bf16[8,576,128]{2,1,0:T(8,128)(2,1)} %get-tuple-element.52), calls=%async_computation.1 | async-start | bytes 2359296 | tf_op jit(solution)/shard_map/all_to_all | solution.py:403
  57.0 10.6 %attend.3 = (bf16[640,128]{1,0:T(8,128)(2,1)}, bf16[384,128]{1,0:T(8,128)(2,1)}, bf16[640,128]{1,0:T(8,128)(2,1)}, bf16[384,128]{1,0:T(8,128)(2,1)}, bf16[640,12...) custom-call(bf16[8,512,128]{2,1,0:T(8,128)(2,1)} %copy-done.3, ...), custom_call_target="tpu_custom_call" | custom-call | flops 6851395584 | bytes 1835008 | tf_op jit(solution)/shard_map/attend/pallas_call | solution.py:391
  67.6 5.0 %all-to-all-done.1.first_ref = bf16[8,576,128]{2,1,0:T(8,128)(2,1)S(1)} async-done(((bf16[8,576,128]{2,1,0:T(8,128)(2,1)}), bf16[8,576,128]{2,1,0:T(8,128)(2,1)S(1)}, u32[]{:S(2)}, u32[]{:S(2)}) %all-to-all-start.1) | async-done | bytes 1179680 | tf_op jit(solution)/shard_map/all_to_all | solution.py:403
  72.6 1.9 %collective-permute-start.2 = (bf16[384,128]{1,0:T(8,128)(2,1)}, bf16[384,128]{1,0:T(8,128)(2,1)S(1)}, u32[]{:S(2)}, u32[]{:S(2)}) collective-permute-start(bf16[384,128]{1,0:T(8,128)(2,1)} %get-tuple-element.68), channel_id=1, source_target_pairs={{0,7},{1,6},{2,1},{3,0},{4,3},{5,2},{6,5},{7,4},{8,15},{9,14},{10,... | collective-permute-start | bytes 294920 | tf_op jit(solution)/shard_map/ppermute | solution.py:471
  74.6 0.9 collective-permute-start.1
  75.4 1.7 %collective-permute-start.3 = (bf16[640,128]{1,0:T(8,128)(2,1)}, bf16[640,128]{1,0:T(8,128)(2,1)S(1)}, u32[]{:S(2)}, u32[]{:S(2)}) collective-permute-start(bf16[640,128]{1,0:T(8,128)(2,1)} %get-tuple-element.69), channel_id=1, source_target_pairs={{0,4},{1,5},{2,6},{3,7},{4,0},{5,1},{6,2},{7,3},{8,12},{9,13},{10,... | collective-permute-start | bytes 491528 | tf_op jit(solution)/shard_map/ppermute | solution.py:471
  77.4 3.4 %collective-permute-start.4 = (bf16[384,128]{1,0:T(8,128)(2,1)}, bf16[384,128]{1,0:T(8,128)(2,1)S(1)}, u32[]{:S(2)}, u32[]{:S(2)}) collective-permute-start(bf16[384,128]{1,0:T(8,128)(2,1)} %get-tuple-element.70), channel_id=1, source_target_pairs={{0,5},{1,4},{2,7},{3,6},{4,1},{5,0},{6,3},{7,2},{8,13},{9,12},{10,... | collective-permute-start | bytes 294920 | tf_op jit(solution)/shard_map/ppermute | solution.py:471
  81.2 0.7 constant_dynamic-slice_fusion.cond_ref
  81.9 6.0 %collective-permute-done.4.refs_5_ = bf16[384,128]{1,0:T(8,128)(2,1)S(1)} collective-permute-done((bf16[384,128]{1,0:T(8,128)(2,1)}, bf16[384,128]{1,0:T(8,128)(2,1)S(1)}, u32[]{:S(2)}, u32[]{:S(2)}) %collective-permute-start.4) | collective-permute-done | bytes 98336 | tf_op jit(solution)/shard_map/ppermute | solution.py:471
  87.9 1.4 %collective-permute-done.6.refs_7_ = bf16[384,128]{1,0:T(8,128)(2,1)S(1)} collective-permute-done((bf16[384,128]{1,0:T(8,128)(2,1)}, bf16[384,128]{1,0:T(8,128)(2,1)S(1)}, u32[]{:S(2)}, u32[]{:S(2)}) %collective-permute-start.6) | collective-permute-done | bytes 98336 | tf_op jit(solution)/shard_map/ppermute | solution.py:471
  89.3 0.7 copy-done.4
  90.1 0.7 copy-done.6
  90.7 2.0 %spread.1 = bf16[32,16,128]{2,1,0:T(8,128)(2,1)} custom-call(s32[1]{0:T(128)} %bitcast.place_ref.refs_4_, bf16[1,608]{1,0:T(2,128)(2,1)} %constant_dynamic-slice_fusion.cond_ref, bf16[640,128]{1,0:T(8,128)(2,1)} %get-tuple-element.73.refs_0_, bf16[640,128]{1,0:T(8,128)(2,1)} %copy-done.4, bf16[640,128]{1,0:T(8,128)(2,1)} %copy-done.5, bf16[640,128]{1,0:T(8,128)(2,1)} %copy-done.6), custom_call_target="tpu_custom_call" | custom-call | tf_op jit(solution)/shard_map/spread/pallas_call | solution.py:391
  92.7 14.3 %all-to-all-start.3 = ((bf16[32,16,128]{2,1,0:T(8,128)(2,1)}), bf16[32,16,128]{2,1,0:T(8,128)(2,1)S(1)}, u32[]{:S(2)}, u32[]{:S(2)}) async-start(bf16[32,16,128]{2,1,0:T(8,128)(2,1)} %spread.1), calls=%async_computation.3 | async-start | bytes 262144 | tf_op jit(solution)/shard_map/all_to_all | solution.py:403
  107.1 4.2 %unpack.1 = (bf16[128,2432]{1,0:T(8,128)(2,1)}, bf16[128,2432]{1,0:T(8,128)(2,1)}, bf16[128,2432]{1,0:T(8,128)(2,1)}, bf16[32,1216]{1,0:T(8,128)(2,1)}, bf16[32,...) custom-call(s32[1]{0:T(128)} %bitcast.place_ref.refs_4_, bf16[8,576,128]{2,1,0:T(8,128)(2,1)} %copy-done.1, ...), custom_call_target="tpu_custom_call" | custom-call | tf_op jit(solution)/shard_map/unpack/pallas_call | solution.py:391
  111.2 6.3 %all-to-all-done.3.in_ref = bf16[32,16,128]{2,1,0:T(8,128)(2,1)S(1)} async-done(((bf16[32,16,128]{2,1,0:T(8,128)(2,1)}), bf16[32,16,128]{2,1,0:T(8,128)(2,1)S(1)}, u32[]{:S(2)}, u32[]{:S(2)}) %all-to-all-start.3) | async-done | bytes 131104 | tf_op jit(solution)/shard_map/all_to_all | solution.py:403
  118.2 3.2 %modulation.1 = f32[608,1216]{1,0:T(8,128)} custom-call(bf16[32,16,128]{2,1,0:T(8,128)(2,1)} %copy-done.7), custom_call_target="tpu_custom_call" | custom-call | tf_op jit(solution)/shard_map/modulation/pallas_call | solution.py:391
  (33 shorter events, 1.5 us)
Async XLA Ops:
  0.6 80.6 %copy-start = (bf16[1,2432]{1,0:T(2,128)(2,1)S(1)}, bf16[1,2432]{1,0:T(2,128)(2,1)}, u32[]{:S(2)}) copy-start(bf16[1,2432]{1,0:T(2,128)(2,1)} %param.22) | copy-start | bytes 14596
  4.1 28.9 %all-to-all-start = ((bf16[8,768,128]{2,1,0:T(8,128)(2,1)}), bf16[8,768,128]{2,1,0:T(8,128)(2,1)S(1)}, u32[]{:S(2)}, u32[]{:S(2)}) async-start(bf16[8,768,128]{2,1,0:T(8,128)(2,1)} %get-tuple-element.48), calls=%async_computation | async-start | bytes 3145728 | tf_op jit(solution)/shard_map/all_to_all | solution.py:403
  10.0 3.0 %copy-start.12 = (f32[4,64]{1,0:T(4,128)S(1)}, f32[4,64]{1,0:T(4,128)}, u32[]{:S(2)}) copy-start(f32[4,64]{1,0:T(4,128)} %param.23) | copy-start | bytes 3076
  33.1 3.6 %copy-start.2 = (bf16[8,768,128]{2,1,0:T(8,128)(2,1)}, bf16[8,768,128]{2,1,0:T(8,128)(2,1)S(1)}, u32[]{:S(2)}) copy-start(bf16[8,768,128]{2,1,0:T(8,128)(2,1)S(1)} %all-to-all-done.refs_0_) | copy-start | bytes 4718596
  33.1 18.9 %all-to-all-start.2 = ((bf16[8,512,128]{2,1,0:T(8,128)(2,1)}), bf16[8,512,128]{2,1,0:T(8,128)(2,1)S(1)}, u32[]{:S(2)}, u32[]{:S(2)}) async-start(bf16[8,512,128]{2,1,0:T(8,128)(2,1)} %pack.2), calls=%async_computation.2 | async-start | bytes 2097152 | tf_op jit(solution)/shard_map/all_to_all | solution.py:403
  51.9 5.1 %copy-start.3 = (bf16[8,512,128]{2,1,0:T(8,128)(2,1)}, bf16[8,512,128]{2,1,0:T(8,128)(2,1)S(1)}, u32[]{:S(2)}) copy-start(bf16[8,512,128]{2,1,0:T(8,128)(2,1)S(1)} %all-to-all-done.2.refs_0_) | copy-start | bytes 3145732
  51.9 20.7 %all-to-all-start.1 = ((bf16[8,576,128]{2,1,0:T(8,128)(2,1)}), bf16[8,576,128]{2,1,0:T(8,128)(2,1)S(1)}, u32[]{:S(2)}, u32[]{:S(2)}) async-start(bf16[8,576,128]{2,1,0:T(8,128)(2,1)} %get-tuple-element.52), calls=%async_computation.1 | async-start | bytes 2359296 | tf_op jit(solution)/shard_map/all_to_all | solution.py:403
  72.6 34.4 %copy-start.1 = (bf16[8,576,128]{2,1,0:T(8,128)(2,1)}, bf16[8,576,128]{2,1,0:T(8,128)(2,1)S(1)}, u32[]{:S(2)}) copy-start(bf16[8,576,128]{2,1,0:T(8,128)(2,1)S(1)} %all-to-all-done.1.first_ref) | copy-start | bytes 3538948
  72.6 4.7 %collective-permute-start = (bf16[384,128]{1,0:T(8,128)(2,1)}, bf16[384,128]{1,0:T(8,128)(2,1)S(1)}, u32[]{:S(2)}, u32[]{:S(2)}) collective-permute-start(bf16[384,128]{1,0:T(8,128)(2,1)} %get-tuple-element.66), channel_id=1, source_target_pairs={{0,1},{1,0},{2,3},{3,2},{4,5},{5,4},{6,7},{7,6},{8,9},{9,8},{10,11... | collective-permute-start | bytes 294920 | tf_op jit(solution)/shard_map/ppermute | solution.py:471
  72.6 8.2 %collective-permute-start.2 = (bf16[384,128]{1,0:T(8,128)(2,1)}, bf16[384,128]{1,0:T(8,128)(2,1)S(1)}, u32[]{:S(2)}, u32[]{:S(2)}) collective-permute-start(bf16[384,128]{1,0:T(8,128)(2,1)} %get-tuple-element.68), channel_id=1, source_target_pairs={{0,7},{1,6},{2,1},{3,0},{4,3},{5,2},{6,5},{7,4},{8,15},{9,14},{10,... | collective-permute-start | bytes 294920 | tf_op jit(solution)/shard_map/ppermute | solution.py:471
  74.6 14.7 %collective-permute-start.1 = (bf16[640,128]{1,0:T(8,128)(2,1)}, bf16[640,128]{1,0:T(8,128)(2,1)S(1)}, u32[]{:S(2)}, u32[]{:S(2)}) collective-permute-start(bf16[640,128]{1,0:T(8,128)(2,1)} %get-tuple-element.67), channel_id=1, source_target_pairs={{0,6},{1,7},{2,0},{3,1},{4,2},{5,3},{6,4},{7,5},{8,14},{9,15},{10,... | collective-permute-start | bytes 491528 | tf_op jit(solution)/shard_map/ppermute | solution.py:471
  75.4 13.9 %collective-permute-start.3 = (bf16[640,128]{1,0:T(8,128)(2,1)}, bf16[640,128]{1,0:T(8,128)(2,1)S(1)}, u32[]{:S(2)}, u32[]{:S(2)}) collective-permute-start(bf16[640,128]{1,0:T(8,128)(2,1)} %get-tuple-element.69), channel_id=1, source_target_pairs={{0,4},{1,5},{2,6},{3,7},{4,0},{5,1},{6,2},{7,3},{8,12},{9,13},{10,... | collective-permute-start | bytes 491528 | tf_op jit(solution)/shard_map/ppermute | solution.py:471
  77.1 12.3 %collective-permute-start.5 = (bf16[640,128]{1,0:T(8,128)(2,1)}, bf16[640,128]{1,0:T(8,128)(2,1)S(1)}, u32[]{:S(2)}, u32[]{:S(2)}) collective-permute-start(bf16[640,128]{1,0:T(8,128)(2,1)} %get-tuple-element.71), channel_id=1, source_target_pairs={{0,2},{1,3},{2,4},{3,5},{4,6},{5,7},{6,0},{7,1},{8,10},{9,11},{10,... | collective-permute-start | bytes 491528 | tf_op jit(solution)/shard_map/ppermute | solution.py:471
  77.4 29.6 %copy-start.8 = (bf16[384,128]{1,0:T(8,128)(2,1)}, bf16[384,128]{1,0:T(8,128)(2,1)S(1)}, u32[]{:S(2)}) copy-start(bf16[384,128]{1,0:T(8,128)(2,1)S(1)} %collective-permute-done.refs_1_) | copy-start | bytes 294916
  77.4 10.5 %collective-permute-start.4 = (bf16[384,128]{1,0:T(8,128)(2,1)}, bf16[384,128]{1,0:T(8,128)(2,1)S(1)}, u32[]{:S(2)}, u32[]{:S(2)}) collective-permute-start(bf16[384,128]{1,0:T(8,128)(2,1)} %get-tuple-element.70), channel_id=1, source_target_pairs={{0,5},{1,4},{2,7},{3,6},{4,1},{5,0},{6,3},{7,2},{8,13},{9,12},{10,... | collective-permute-start | bytes 294920 | tf_op jit(solution)/shard_map/ppermute | solution.py:471
  80.8 26.2 %copy-start.9 = (bf16[384,128]{1,0:T(8,128)(2,1)}, bf16[384,128]{1,0:T(8,128)(2,1)S(1)}, u32[]{:S(2)}) copy-start(bf16[384,128]{1,0:T(8,128)(2,1)S(1)} %collective-permute-done.2.refs_3_) | copy-start | bytes 294916
  80.8 8.5 %collective-permute-start.6 = (bf16[384,128]{1,0:T(8,128)(2,1)}, bf16[384,128]{1,0:T(8,128)(2,1)S(1)}, u32[]{:S(2)}, u32[]{:S(2)}) collective-permute-start(bf16[384,128]{1,0:T(8,128)(2,1)} %get-tuple-element.72), channel_id=1, source_target_pairs={{0,3},{1,2},{2,5},{3,4},{4,7},{5,6},{6,1},{7,0},{8,11},{9,10},{10,... | collective-permute-start | bytes 294920 | tf_op jit(solution)/shard_map/ppermute | solution.py:471
  87.9 19.1 %copy-start.10 = (bf16[384,128]{1,0:T(8,128)(2,1)}, bf16[384,128]{1,0:T(8,128)(2,1)S(1)}, u32[]{:S(2)}) copy-start(bf16[384,128]{1,0:T(8,128)(2,1)S(1)} %collective-permute-done.4.refs_5_) | copy-start | bytes 294916
  89.3 17.7 %copy-start.11 = (bf16[384,128]{1,0:T(8,128)(2,1)}, bf16[384,128]{1,0:T(8,128)(2,1)S(1)}, u32[]{:S(2)}) copy-start(bf16[384,128]{1,0:T(8,128)(2,1)S(1)} %collective-permute-done.6.refs_7_) | copy-start | bytes 294916
  89.3 0.7 copy-start.4
  89.3 0.8 copy-start.5
  90.1 0.7 copy-start.6
  92.7 24.9 %all-to-all-start.3 = ((bf16[32,16,128]{2,1,0:T(8,128)(2,1)}), bf16[32,16,128]{2,1,0:T(8,128)(2,1)S(1)}, u32[]{:S(2)}, u32[]{:S(2)}) async-start(bf16[32,16,128]{2,1,0:T(8,128)(2,1)} %spread.1), calls=%async_computation.3 | async-start | bytes 262144 | tf_op jit(solution)/shard_map/all_to_all | solution.py:403
  117.6 0.7 copy-start.7

commit v2 on v1

--- a/solution.py
+++ b/solution.py
@@ -54,45 +54,30 @@
     return ((place // 2 + blocks + way * (index // 2)) % blocks) * 2 + (place + index) % 2
 
 
-def pack_kernel(
-    half_heads,
-    chunks,
-    place_ref,
-    iq_ref,
-    ik_ref,
-    iv_ref,
-    ic_ref,
-    tq_ref,
-    tk_ref,
-    tv_ref,
-    tc_ref,
-    ig_ref,
-    tg_ref,
-    *out_refs,
-):
-    send_refs, kept_refs = out_refs[: len(chunks)], out_refs[len(chunks) :]
-
+def pack_kernel(half_heads, slots, place_ref, iq_ref, ik_ref, iv_ref, ic_ref, *refs):
     def columns(ref, head):
         return ref[:, head * HEAD : (head + 1) * HEAD]
 
     rows = iq_ref.shape[0]
-    for slots, send_ref in zip(chunks, send_refs):
-        for dest in range(send_ref.shape[0]):
-            for position, slot in enumerate(slots):
-                head = head_of(dest, slot, half_heads)
-                for pair, (first, second) in enumerate(((iq_ref, ik_ref), (iv_ref, ic_ref))):
-                    tile = (
-                        jnp.zeros((rows, PAIR), bf16)
-                        if head is None
-                        else jnp.concatenate([columns(first, head), columns(second, head)], 1)
-                    )
-                    start = (2 * position + pair) * rows
-                    send_ref[dest, start : start + rows, :] = tile
-    if not kept_refs:
+    if len(refs) == 1:
+        (send_ref,) = refs
+    else:
+        tq_ref, tk_ref, tv_ref, tc_ref, ig_ref, tg_ref, send_ref, text_ref, gate_ref = refs
+    for dest in range(send_ref.shape[0]):
+        for position, slot in enumerate(slots):
+            head = head_of(dest, slot, half_heads)
+            for pair, (first, second) in enumerate(((iq_ref, ik_ref), (iv_ref, ic_ref))):
+                tile = (
+                    jnp.zeros((rows, PAIR), bf16)
+                    if head is None
+                    else jnp.concatenate([columns(first, head), columns(second, head)], 1)
+                )
+                start = (2 * position + pair) * rows
+                send_ref[dest, start : start + rows, :] = tile
+    if len(refs) == 1:
         return
-    text_ref, gate_ref = kept_refs
     place = place_ref[0]
-    for device in range(send_refs[0].shape[0]):
+    for device in range(send_ref.shape[0]):
 
         @pl.when(place == device)
         def _():
@@ -121,7 +106,7 @@
     if first:
         out_ref, pay_ref, sum_ref = refs
     else:
-        out_refs = refs
+        out_refs, sum_ref = refs[:-1], refs[-1]
     devices, tile_rows = in_ref.shape[0], in_ref.shape[1] // (2 * count)
     rows, txt = devices * tile_rows, text_ref.shape[0]
     total_rows = rows + txt
@@ -224,12 +209,13 @@
         pair_grad = (inv * scaled - raw[head] * (inv * inv * inv) * mean).astype(bf16)
         value_grad = value_key_grad[head][:, :HEAD].astype(bf16)
         begin = (count + head // 2) * tile_rows
+        pair_at = head * tile_rows
         pairs = pair_grad[:rows].reshape(devices, tile_rows, PAIR)
         tiles = value_grad[:rows].reshape(devices, tile_rows, HEAD)
         targets = [(out_ref, slice(None))] if first else [(r, i) for i, r in enumerate(out_refs)]
         for ref, device in targets:
             value = tiles[device]
-            ref[..., head * tile_rows : (head + 1) * tile_rows, :] = pairs[device]
+            ref[..., pair_at : pair_at + tile_rows, :] = pairs[device]
             if head % 2 == 1:
                 ref[..., begin : begin + tile_rows, HEAD:] = value
             elif head < count - 1:
@@ -252,20 +238,20 @@
         return
     packed = [part.astype(f32) for part in split_three(jnp.concatenate(sums, 0))]
     packed = jnp.concatenate(packed + [jnp.zeros((GATE_ROWS - 3 * SLOTS, PAIR), f32)], 0)
-    pay = jnp.concatenate([earlier_pay_ref[...]] + text_tiles + [packed.astype(bf16)], 0)
+    sum_ref[...] = packed.astype(bf16)
+    pay = jnp.concatenate([earlier_pay_ref[...]] + text_tiles, 0)
     for ref in out_refs[::2]:
         ref[ref.shape[0] - pay.shape[0] :, :] = pay
 
 
-def pay_of(ref):
-    start = ref.shape[0] - SLOTS * TEXT_ROWS - GATE_ROWS
-    packed = ref[start + SLOTS * TEXT_ROWS :, :].astype(f32)
-    return start, packed[:SLOTS] + packed[SLOTS : 2 * SLOTS] + packed[2 * SLOTS : 3 * SLOTS]
+def sums_of(ref):
+    packed = ref[...].astype(f32)
+    return packed[:SLOTS] + packed[SLOTS : 2 * SLOTS] + packed[2 * SLOTS : 3 * SLOTS]
 
 
 def spread_kernel(half_heads, place_ref, cond_ref, *refs):
-    pay_refs, out_ref = refs[:-1], refs[-1]
-    blocks = len(pay_refs)
+    sum_refs, out_ref = refs[:-1], refs[-1]
+    blocks = len(sum_refs)
     cond = cond_ref[...].astype(f32)
     for place in range(blocks):
 
@@ -274,7 +260,7 @@
             heads = []
             for block in range(blocks):
                 used = min(SLOTS, half_heads - block * SLOTS)
-                sums = pay_of(pay_refs[(block - place) % blocks])[1]
+                sums = sums_of(sum_refs[(block - place) % blocks])
                 heads += [sums[slot : slot + 1, :HEAD] for slot in range(used)]
             rows = []
             for row in (jnp.concatenate(heads, 1), cond):
@@ -308,15 +294,15 @@
 
 
 def unpack_kernel(half_heads, chunks, place_ref, first_ref, *refs):
-    routed_refs, outs = refs[:ROUTES], refs[ROUTES:]
+    blocks = ROUTES // 2
+    routed_refs, sum_refs, outs = refs[:ROUTES], refs[ROUTES : ROUTES + blocks], refs[ROUTES + blocks :]
     q_ref, k_ref, v_ref, tq_ref, tk_ref, tv_ref, tg_ref, held_ref = outs
     for index, ref in enumerate(routed_refs):
         held_ref[route(place_ref[0], index)] = ref[: held_ref.shape[1], :]
-    back_refs = (first_ref, held_ref)
     rows = q_ref.shape[0]
     half = rows // 2
     pieces = {}
-    for slots, back_ref in zip(chunks, back_refs):
+    for slots, back_ref in zip(chunks, (first_ref, held_ref)):
         count = len(slots)
         for source in range(back_ref.shape[0]):
             for position, slot in enumerate(slots):
@@ -341,8 +327,8 @@
     txt = tq_ref.shape[0]
     pay_refs = routed_refs[::2]
 
-    def place_text(block, pay_ref):
-        start, sums = pay_of(pay_ref)
+    def place_text(block, pay_ref, sum_ref):
+        start, sums = held_ref.shape[1], sums_of(sum_ref)
         for slot in range(min(SLOTS, half_heads - block * SLOTS)):
             head = block * SLOTS + slot
             lanes = slice(head * HEAD, (head + 1) * HEAD)
@@ -354,13 +340,12 @@
             tv_ref[:, lanes] = jnp.concatenate([folded[:, :HEAD], folded[:, HEAD:]], 0)
             tg_ref[:, lanes] = sums[slot : slot + 1, HEAD:]
 
-    blocks = len(pay_refs)
     for shift in range(blocks):
         for block in range(blocks):
 
             @pl.when(place_ref[0] // 2 == (block - shift) % blocks)
             def _():
-                place_text(block, pay_refs[shift])
+                place_text(block, pay_refs[shift], sum_refs[shift])
 
 
 def shards(
@@ -404,22 +389,25 @@
 
     image = (img_query[0], img_key[0], img_value[0], img_cotangent[0])
     text = (txt_query[0], txt_key[0], txt_value[0], txt_cotangent[0])
-    operands = (place[None], *image, *text, img_gate, txt_gate)
     sends = []
-    kept = None
     for slots in CHUNKS:
         outs = [shape((devices, 2 * len(slots) * rows, PAIR), bf16)]
-        if kept is None:
+        if slots[-1] == SLOTS - 1:
             outs += [
                 shape((txt, 2 * SLOTS * PAIR), bf16),
                 shape((SLOTS, 2, PAIR), f32),
             ]
-        send, *others = call(
-            functools.partial(pack_kernel, half_heads, (slots,)), outs, operands, "pack", smem=1
+            operands = (*image, *text, img_gate, txt_gate)
+        else:
+            operands = image
+        send, *kept = call(
+            functools.partial(pack_kernel, half_heads, slots),
+            outs,
+            (place[None], *operands),
+            "pack",
+            smem=1,
         )
         sends.append(send)
-        if kept is None:
-            kept = others
     text_rows, gates = kept
     gains = norm_gains.reshape(2, PAIR)
 
@@ -438,7 +426,7 @@
     for slots, arrived in zip(CHUNKS, received):
         count = len(slots)
         last = slots[-1] == SLOTS - 1
-        pay_rows = (slots[-1] + 1) * TEXT_ROWS + (GATE_ROWS if last else 0)
+        pay_rows = (slots[-1] + 1) * TEXT_ROWS
         outs = [
             shape((devices, 3 * count * rows // 2, PAIR), bf16),
             shape((pay_rows, PAIR), bf16),
@@ -448,7 +436,7 @@
             outs = [
                 shape((3 * count * rows // 2 + (0 if index % 2 else pay_rows), PAIR), bf16)
                 for index in range(ROUTES)
-            ]
+            ] + [shape((GATE_ROWS, PAIR), bf16)]
         cost = pl.CostEstimate(
             flops=count * 12 * total_rows * total_rows * HEAD * 4,
             bytes_accessed=count * devices * rows * HEAD * 14,
@@ -464,33 +452,39 @@
         if not last:
             earlier = (place[None], *back[1:])
             back_first = exchange(back[0], ("blk", "uly"))
-    back_first, *back = lax.optimization_barrier((back_first, *back))
-    routed = [back[0]]
-    for index in range(1, ROUTES):
+    *back, own_sums = back
+
+    def step_back(operand, index):
         pairs = [(device, route(device, index, -1)) for device in range(devices)]
-        routed.append(lax.ppermute(back[index], ("blk", "uly"), pairs))
-    routed = lax.optimization_barrier(routed)
+        return lax.ppermute(operand, ("blk", "uly"), pairs)
+
+    sums = [own_sums] + [step_back(own_sums, index) for index in range(2, ROUTES, 2)]
+    *back, sums = lax.optimization_barrier((*back, sums))
+    routed = [back[0]] + [step_back(back[index], index) for index in range(1, ROUTES)]
     tile_rows = -(-(pl.cdiv(half_width, PAIR) + pl.cdiv(width_rows, PAIR)) // 16) * 16
     (gate_rows,) = call(
         functools.partial(spread_kernel, half_heads),
         [shape((samples, tile_rows, PAIR), bf16)],
-        (place[None], cond_row, *routed[::2]),
+        (place[None], cond_row, *sums),
         "spread",
         smem=1,
     )
+    gate_rows, back_first = lax.optimization_barrier((gate_rows, back_first))
+    gate_all = exchange(gate_rows, "dp")
     (modulation_grad,) = call(
         modulation_kernel,
         [shape((width_rows, half_width), f32)],
-        (exchange(gate_rows, "dp"),),
+        (gate_all,),
         "modulation",
         scratch=[pltpu.VMEM((samples * tile_rows, PAIR), f32)],
     )
+    modulation_grad, *routed = lax.optimization_barrier((modulation_grad, *routed))
     out_query, out_key, out_value, tq_grad, tk_grad, tv_grad, txt_gate_grad = call(
         functools.partial(unpack_kernel, half_heads, CHUNKS),
         [shape((rows, width), bf16)] * 3
         + [shape((txt, half_width), bf16)] * 3
         + [shape((1, half_width), f32)],
-        (place[None], back_first, *routed),
+        (place[None], back_first, *routed, *sums),
         "unpack",
         smem=1,
         scratch=[pltpu.VMEM((devices, 3 * len(CHUNKS[1]) * rows // 2, PAIR), bf16)],

time: 122 us -> 117 us (0.959)
  waiting for transfers between devices: 38.4 us -> 29.4 us
  starting transfers between devices: 37.1 us -> 40.9 us
    all_to_all x4, waiting for transfers between devices: 30.7 us -> 20.8 us  [exchange(): return lax.all_to_all(operand, axes, 0, 0, tiled=True)]
    ppermute x7 -> x10, starting transfers between devices: 8.3 us -> 11.4 us  [step_back(): return lax.ppermute(operand, ('blk', 'uly'), pairs)]
    ppermute x7 -> x10, waiting for transfers between devices: 7.7 us -> 8.6 us  [step_back(): return lax.ppermute(operand, ('blk', 'uly'), pairs)]
    unnamed x26 -> x32, local copies, waits for them, and re-layouts: 2.09 us -> 2.65 us
  transfers between devices with their start and end apart: 11 -> 14, of which waited for: 6 -> 7; matrix products, arithmetic and copies ran while one was open for 1% -> 1% of each run, Pallas kernels for 27% -> 29%
where the time goes in v2:
time: 117 us; the launch traced here: 116 us
  Pallas kernels  41.2 us (35%)
  starting transfers between devices  40.9 us (35%)
  waiting for transfers between devices  29.4 us (25%)
  local copies, waits for them, and re-layouts  3.9 us (3%)
    pallas_call x7, Pallas kernels, call(): pl.pallas_call(kernel, in_specs=[pl.BlockSpec(memory_space=pltpu.SMEM)] *...  41.2 us
    all_to_all x4, starting transfers between devices, exchange(): return lax.all_to_all(operand, axes, 0, 0, tiled=True)  29.5 us
    all_to_all x4, waiting for transfers between devices, exchange(): return lax.all_to_all(operand, axes, 0, 0, tiled=True)  20.8 us
    ppermute x10, starting transfers between devices, step_back(): return lax.ppermute(operand, ('blk', 'uly'), pairs)  11.4 us
    ppermute x10, waiting for transfers between devices, step_back(): return lax.ppermute(operand, ('blk', 'uly'), pairs)  8.6 us
    unnamed x32, local copies, waits for them, and re-layouts  2.65 us
  transfers between devices with their start and end apart: 14, of which 7 were waited for; matrix products, arithmetic and copies ran while one was open for 1% of the time, Pallas kernels for 29%

profile of v2, /device:TPU:1, one launch (start us, length us, event | category | flops | bytes accessed | tf_op | source)
XLA Modules:
  0.0 116.2 jit_solution(9506638744643023747)
XLA Ops:
  0.7 3.3 %pack.3 = bf16[8,768,128]{2,1,0:T(8,128)(2,1)} custom-call(s32[1]{0:T(128)} %bitcast.place_ref.refs_4_, bf16[128,2432]{1,0:T(8,128)(2,1)} %bitcast.15, bf16[128,2432]{1,0:T(8,128)(2,1)} %bitcast.17, bf16[128,2432]{1,0:T(8,128)(2,1)} %bitcast.19, bf16[128,2432]{1,0:T(8,128)(2,1)} %bitcast.21), custom_call_target="tpu_custom_call" | custom-call | tf_op jit(solution)/shard_map/pack/pallas_call | solution.py:376
  3.9 6.0 %all-to-all-start = ((bf16[8,768,128]{2,1,0:T(8,128)(2,1)}), bf16[8,768,128]{2,1,0:T(8,128)(2,1)S(1)}, u32[]{:S(2)}, u32[]{:S(2)}) async-start(bf16[8,768,128]{2,1,0:T(8,128)(2,1)} %pack.3), calls=%async_computation | async-start | bytes 3145728 | tf_op jit(solution)/shard_map/all_to_all | solution.py:388
  10.5 3.1 %pack.2 = (bf16[8,512,128]{2,1,0:T(8,128)(2,1)}, bf16[32,1280]{1,0:T(8,128)(2,1)}, f32[5,2,128]{2,1,0:T(2,128)}) custom-call(s32[1]{0:T(128)} %bitcast.place_ref.refs_4_, bf16[128,2432]{1,0:T(8,128)(2,1)} %bitcast.16, bf16[128,2432]{1,0:T(8,128)(2,1)} %bitcast.18, bf16[128,2432]{1,0:T(8,128)(2,1)} %bitcast.20, bf16[128,2432]{1,0:T(8,128)(2,1)} %bitcast.22, ...), custom_call_target="tpu_custom_call" | custom-call | tf_op jit(solution)/shard_map/pack/pallas_call | solution.py:376
  13.7 19.3 %all-to-all-done.refs_0_ = bf16[8,768,128]{2,1,0:T(8,128)(2,1)S(1)} async-done(((bf16[8,768,128]{2,1,0:T(8,128)(2,1)}), bf16[8,768,128]{2,1,0:T(8,128)(2,1)S(1)}, u32[]{:S(2)}, u32[]{:S(2)}) %all-to-all-start) | async-done | bytes 1572896 | tf_op jit(solution)/shard_map/all_to_all | solution.py:388
  33.0 3.6 %all-to-all-start.1 = ((bf16[8,512,128]{2,1,0:T(8,128)(2,1)}), bf16[8,512,128]{2,1,0:T(8,128)(2,1)S(1)}, u32[]{:S(2)}, u32[]{:S(2)}) async-start(bf16[8,512,128]{2,1,0:T(8,128)(2,1)} %get-tuple-element.56), calls=%async_computation.1 | async-start | bytes 2097152 | tf_op jit(solution)/shard_map/all_to_all | solution.py:388
  36.5 15.3 %attend.2 = (bf16[8,576,128]{2,1,0:T(8,128)(2,1)}, bf16[144,128]{1,0:T(8,128)(2,1)}, f32[8,128]{1,0:T(8,128)}) custom-call(bf16[8,768,128]{2,1,0:T(8,128)(2,1)} %copy-done.2, bf16[32,1280]{1,0:T(8,128)(2,1)} %get-tuple-element.57.refs_1_, f32[2,128]{1,0:T(2,128)} %reshape.19.refs_2_, f32[5,2,128]{2,1,0:T(2,128)} %get-tuple-element.58.refs_3_), custom_call_target="tpu_custom_call" | custom-call | flops 10277093376 | bytes 2752512 | tf_op jit(solution)/shard_map/attend/pallas_call | solution.py:376
  51.8 5.1 %all-to-all-start.2 = ((bf16[8,576,128]{2,1,0:T(8,128)(2,1)}), bf16[8,576,128]{2,1,0:T(8,128)(2,1)S(1)}, u32[]{:S(2)}, u32[]{:S(2)}) async-start(bf16[8,576,128]{2,1,0:T(8,128)(2,1)} %get-tuple-element.75), calls=%async_computation.2 | async-start | bytes 2359296 | tf_op jit(solution)/shard_map/all_to_all | solution.py:388
  56.9 10.6 %attend.3 = (bf16[624,128]{1,0:T(8,128)(2,1)}, bf16[384,128]{1,0:T(8,128)(2,1)}, bf16[624,128]{1,0:T(8,128)(2,1)}, bf16[384,128]{1,0:T(8,128)(2,1)}, bf16[624,12...) custom-call(bf16[8,512,128]{2,1,0:T(8,128)(2,1)} %copy-done.3, ...), custom_call_target="tpu_custom_call" | custom-call | flops 6851395584 | bytes 1835008 | tf_op jit(solution)/shard_map/attend/pallas_call | solution.py:376
  67.5 1.4 %collective-permute-start.2 = (bf16[16,128]{1,0:T(8,128)(2,1)}, bf16[16,128]{1,0:T(8,128)(2,1)S(1)}, u32[]{:S(2)}, u32[]{:S(2)}) collective-permute-start(bf16[16,128]{1,0:T(8,128)(2,1)} %get-tuple-element.71.refs_0_.refs_8_), channel_id=1, source_target_pairs={{0,2},{1,3},{2,4},{3,5},{4,6},{5,7},{6,0},{7,1},{8,10},{9,11},{10,... | collective-permute-start | bytes 12296 | tf_op jit(solution)/shard_map/ppermute | solution.py:459
  69.0 2.4 %collective-permute-start.1 = (bf16[16,128]{1,0:T(8,128)(2,1)}, bf16[16,128]{1,0:T(8,128)(2,1)S(1)}, u32[]{:S(2)}, u32[]{:S(2)}) collective-permute-start(bf16[16,128]{1,0:T(8,128)(2,1)} %get-tuple-element.71.refs_0_.refs_8_), channel_id=1, source_target_pairs={{0,4},{1,5},{2,6},{3,7},{4,0},{5,1},{6,2},{7,3},{8,12},{9,13},{10,... | collective-permute-start | bytes 12296 | tf_op jit(solution)/shard_map/ppermute | solution.py:459
  71.4 1.2 %collective-permute-start = (bf16[16,128]{1,0:T(8,128)(2,1)}, bf16[16,128]{1,0:T(8,128)(2,1)S(1)}, u32[]{:S(2)}, u32[]{:S(2)}) collective-permute-start(bf16[16,128]{1,0:T(8,128)(2,1)} %get-tuple-element.71.refs_0_.refs_8_), channel_id=1, source_target_pairs={{0,6},{1,7},{2,0},{3,1},{4,2},{5,3},{6,4},{7,5},{8,14},{9,15},{10,... | collective-permute-start | bytes 12296 | tf_op jit(solution)/shard_map/ppermute | solution.py:459
  73.5 0.8 collective-permute-done.refs_1_.refs_9_
  74.9 1.5 %spread.1 = bf16[32,16,128]{2,1,0:T(8,128)(2,1)} custom-call(s32[1]{0:T(128)} %bitcast.place_ref.refs_4_, bf16[1,608]{1,0:T(2,128)(2,1)} %constant_dynamic-slice_fusion.cond_ref, bf16[16,128]{1,0:T(8,128)(2,1)} %get-tuple-element.71.refs_0_.refs_8_, bf16[16,128]{1,0:T(8,128)(2,1)} %copy-done.14, bf16[16,128]{1,0:T(8,128)(2,1)} %copy-done.13, ...), custom_call_target="tpu_custom_call" | custom-call | tf_op jit(solution)/shard_map/spread/pallas_call | solution.py:376
  76.4 14.8 %all-to-all-start.3 = ((bf16[32,16,128]{2,1,0:T(8,128)(2,1)}), bf16[32,16,128]{2,1,0:T(8,128)(2,1)S(1)}, u32[]{:S(2)}, u32[]{:S(2)}) async-start(bf16[32,16,128]{2,1,0:T(8,128)(2,1)} %spread.1), calls=%async_computation.3 | async-start | bytes 262144 | tf_op jit(solution)/shard_map/all_to_all | solution.py:388
  91.3 0.7 collective-permute-start.3
  91.9 2.9 %collective-permute-start.5 = (bf16[384,128]{1,0:T(8,128)(2,1)}, bf16[384,128]{1,0:T(8,128)(2,1)S(1)}, u32[]{:S(2)}, u32[]{:S(2)}) collective-permute-start(bf16[384,128]{1,0:T(8,128)(2,1)} %get-tuple-element.81), channel_id=1, source_target_pairs={{0,7},{1,6},{2,1},{3,0},{4,3},{5,2},{6,5},{7,4},{8,15},{9,14},{10,... | collective-permute-start | bytes 294920 | tf_op jit(solution)/shard_map/ppermute | solution.py:459
  94.9 0.9 collective-permute-start.6
  96.4 2.6 %collective-permute-done.3.refs_1_ = bf16[384,128]{1,0:T(8,128)(2,1)S(1)} collective-permute-done((bf16[384,128]{1,0:T(8,128)(2,1)}, bf16[384,128]{1,0:T(8,128)(2,1)S(1)}, u32[]{:S(2)}, u32[]{:S(2)}) %collective-permute-start.3) | collective-permute-done | bytes 98336 | tf_op jit(solution)/shard_map/ppermute | solution.py:459
  99.0 1.2 %collective-permute-start.7 = (bf16[384,128]{1,0:T(8,128)(2,1)}, bf16[384,128]{1,0:T(8,128)(2,1)S(1)}, u32[]{:S(2)}, u32[]{:S(2)}) collective-permute-start(bf16[384,128]{1,0:T(8,128)(2,1)} %get-tuple-element.83), channel_id=1, source_target_pairs={{0,5},{1,4},{2,7},{3,6},{4,1},{5,0},{6,3},{7,2},{8,13},{9,12},{10,... | collective-permute-start | bytes 294920 | tf_op jit(solution)/shard_map/ppermute | solution.py:459
  100.3 1.5 %all-to-all-done.3.in_ref = bf16[32,16,128]{2,1,0:T(8,128)(2,1)S(1)} async-done(((bf16[32,16,128]{2,1,0:T(8,128)(2,1)}), bf16[32,16,128]{2,1,0:T(8,128)(2,1)S(1)}, u32[]{:S(2)}, u32[]{:S(2)}) %all-to-all-start.3) | async-done | bytes 131104 | tf_op jit(solution)/shard_map/all_to_all | solution.py:388
  102.5 3.2 %modulation.1 = f32[608,1216]{1,0:T(8,128)} custom-call(bf16[32,16,128]{2,1,0:T(8,128)(2,1)} %copy-done.4), custom_call_target="tpu_custom_call" | custom-call | tf_op jit(solution)/shard_map/modulation/pallas_call | solution.py:376
  105.7 1.3 %collective-permute-done.7.refs_5_ = bf16[384,128]{1,0:T(8,128)(2,1)S(1)} collective-permute-done((bf16[384,128]{1,0:T(8,128)(2,1)}, bf16[384,128]{1,0:T(8,128)(2,1)S(1)}, u32[]{:S(2)}, u32[]{:S(2)}) %collective-permute-start.7) | collective-permute-done | bytes 98336 | tf_op jit(solution)/shard_map/ppermute | solution.py:459
  107.0 3.5 %collective-permute-done.9.refs_7_ = bf16[384,128]{1,0:T(8,128)(2,1)S(1)} collective-permute-done((bf16[384,128]{1,0:T(8,128)(2,1)}, bf16[384,128]{1,0:T(8,128)(2,1)S(1)}, u32[]{:S(2)}, u32[]{:S(2)}) %collective-permute-start.9) | collective-permute-done | bytes 98336 | tf_op jit(solution)/shard_map/ppermute | solution.py:459
  111.9 4.2 %unpack.1 = (bf16[128,2432]{1,0:T(8,128)(2,1)}, bf16[128,2432]{1,0:T(8,128)(2,1)}, bf16[128,2432]{1,0:T(8,128)(2,1)}, bf16[32,1216]{1,0:T(8,128)(2,1)}, bf16[32,...) custom-call(s32[1]{0:T(128)} %bitcast.place_ref.refs_4_, bf16[8,576,128]{2,1,0:T(8,128)(2,1)} %copy-done.1, ...), custom_call_target="tpu_custom_call" | custom-call | tf_op jit(solution)/shard_map/unpack/pallas_call | solution.py:376
  (45 shorter events, 4.9 us)
Async XLA Ops:
  0.6 71.9 %copy-start = (bf16[1,2432]{1,0:T(2,128)(2,1)S(1)}, bf16[1,2432]{1,0:T(2,128)(2,1)}, u32[]{:S(2)}) copy-start(bf16[1,2432]{1,0:T(2,128)(2,1)} %param.22) | copy-start | bytes 14596
  3.9 6.0 %copy-start.15 = (f32[4,64]{1,0:T(4,128)S(1)}, f32[4,64]{1,0:T(4,128)}, u32[]{:S(2)}) copy-start(f32[4,64]{1,0:T(4,128)} %param.23) | copy-start | bytes 3076
  3.9 29.0 %all-to-all-start = ((bf16[8,768,128]{2,1,0:T(8,128)(2,1)}), bf16[8,768,128]{2,1,0:T(8,128)(2,1)S(1)}, u32[]{:S(2)}, u32[]{:S(2)}) async-start(bf16[8,768,128]{2,1,0:T(8,128)(2,1)} %pack.3), calls=%async_computation | async-start | bytes 3145728 | tf_op jit(solution)/shard_map/all_to_all | solution.py:388
  33.0 3.6 %copy-start.2 = (bf16[8,768,128]{2,1,0:T(8,128)(2,1)}, bf16[8,768,128]{2,1,0:T(8,128)(2,1)S(1)}, u32[]{:S(2)}) copy-start(bf16[8,768,128]{2,1,0:T(8,128)(2,1)S(1)} %all-to-all-done.refs_0_) | copy-start | bytes 4718596
  33.0 18.9 %all-to-all-start.1 = ((bf16[8,512,128]{2,1,0:T(8,128)(2,1)}), bf16[8,512,128]{2,1,0:T(8,128)(2,1)S(1)}, u32[]{:S(2)}, u32[]{:S(2)}) async-start(bf16[8,512,128]{2,1,0:T(8,128)(2,1)} %get-tuple-element.56), calls=%async_computation.1 | async-start | bytes 2097152 | tf_op jit(solution)/shard_map/all_to_all | solution.py:388
  51.8 5.1 %copy-start.3 = (bf16[8,512,128]{2,1,0:T(8,128)(2,1)}, bf16[8,512,128]{2,1,0:T(8,128)(2,1)S(1)}, u32[]{:S(2)}) copy-start(bf16[8,512,128]{2,1,0:T(8,128)(2,1)S(1)} %all-to-all-done.1.refs_0_) | copy-start | bytes 3145732
  51.8 24.6 %all-to-all-start.2 = ((bf16[8,576,128]{2,1,0:T(8,128)(2,1)}), bf16[8,576,128]{2,1,0:T(8,128)(2,1)S(1)}, u32[]{:S(2)}, u32[]{:S(2)}) async-start(bf16[8,576,128]{2,1,0:T(8,128)(2,1)} %get-tuple-element.75), calls=%async_computation.2 | async-start | bytes 2359296 | tf_op jit(solution)/shard_map/all_to_all | solution.py:388
  67.5 5.7 %collective-permute-start.2 = (bf16[16,128]{1,0:T(8,128)(2,1)}, bf16[16,128]{1,0:T(8,128)(2,1)S(1)}, u32[]{:S(2)}, u32[]{:S(2)}) collective-permute-start(bf16[16,128]{1,0:T(8,128)(2,1)} %get-tuple-element.71.refs_0_.refs_8_), channel_id=1, source_target_pairs={{0,2},{1,3},{2,4},{3,5},{4,6},{5,7},{6,0},{7,1},{8,10},{9,11},{10,... | collective-permute-start | bytes 12296 | tf_op jit(solution)/shard_map/ppermute | solution.py:459
  69.0 4.6 %collective-permute-start.1 = (bf16[16,128]{1,0:T(8,128)(2,1)}, bf16[16,128]{1,0:T(8,128)(2,1)S(1)}, u32[]{:S(2)}, u32[]{:S(2)}) collective-permute-start(bf16[16,128]{1,0:T(8,128)(2,1)} %get-tuple-element.71.refs_0_.refs_8_), channel_id=1, source_target_pairs={{0,4},{1,5},{2,6},{3,7},{4,0},{5,1},{6,2},{7,3},{8,12},{9,13},{10,... | collective-permute-start | bytes 12296 | tf_op jit(solution)/shard_map/ppermute | solution.py:459
  71.4 3.0 %collective-permute-start = (bf16[16,128]{1,0:T(8,128)(2,1)}, bf16[16,128]{1,0:T(8,128)(2,1)S(1)}, u32[]{:S(2)}, u32[]{:S(2)}) collective-permute-start(bf16[16,128]{1,0:T(8,128)(2,1)} %get-tuple-element.71.refs_0_.refs_8_), channel_id=1, source_target_pairs={{0,6},{1,7},{2,0},{3,1},{4,2},{5,3},{6,4},{7,5},{8,14},{9,15},{10,... | collective-permute-start | bytes 12296 | tf_op jit(solution)/shard_map/ppermute | solution.py:459
  73.2 1.1 copy-start.12
  73.5 0.8 copy-start.13
  76.4 29.3 %copy-start.1 = (bf16[8,576,128]{2,1,0:T(8,128)(2,1)}, bf16[8,576,128]{2,1,0:T(8,128)(2,1)S(1)}, u32[]{:S(2)}) copy-start(bf16[8,576,128]{2,1,0:T(8,128)(2,1)S(1)} %all-to-all-done.2.first_ref) | copy-start | bytes 3538948
  76.4 25.4 %all-to-all-start.3 = ((bf16[32,16,128]{2,1,0:T(8,128)(2,1)}), bf16[32,16,128]{2,1,0:T(8,128)(2,1)S(1)}, u32[]{:S(2)}, u32[]{:S(2)}) async-start(bf16[32,16,128]{2,1,0:T(8,128)(2,1)} %spread.1), calls=%async_computation.3 | async-start | bytes 262144 | tf_op jit(solution)/shard_map/all_to_all | solution.py:388
  91.3 7.7 %collective-permute-start.3 = (bf16[384,128]{1,0:T(8,128)(2,1)}, bf16[384,128]{1,0:T(8,128)(2,1)S(1)}, u32[]{:S(2)}, u32[]{:S(2)}) collective-permute-start(bf16[384,128]{1,0:T(8,128)(2,1)} %get-tuple-element.79), channel_id=1, source_target_pairs={{0,1},{1,0},{2,3},{3,2},{4,5},{5,4},{6,7},{7,6},{8,9},{9,8},{10,11... | collective-permute-start | bytes 294920 | tf_op jit(solution)/shard_map/ppermute | solution.py:459
  91.9 8.3 %collective-permute-start.5 = (bf16[384,128]{1,0:T(8,128)(2,1)}, bf16[384,128]{1,0:T(8,128)(2,1)S(1)}, u32[]{:S(2)}, u32[]{:S(2)}) collective-permute-start(bf16[384,128]{1,0:T(8,128)(2,1)} %get-tuple-element.81), channel_id=1, source_target_pairs={{0,7},{1,6},{2,1},{3,0},{4,3},{5,2},{6,5},{7,4},{8,15},{9,14},{10,... | collective-permute-start | bytes 294920 | tf_op jit(solution)/shard_map/ppermute | solution.py:459
  94.9 15.7 %collective-permute-start.4 = (bf16[624,128]{1,0:T(8,128)(2,1)}, bf16[624,128]{1,0:T(8,128)(2,1)S(1)}, u32[]{:S(2)}, u32[]{:S(2)}) collective-permute-start(bf16[624,128]{1,0:T(8,128)(2,1)} %get-tuple-element.80), channel_id=1, source_target_pairs={{0,6},{1,7},{2,0},{3,1},{4,2},{5,3},{6,4},{7,5},{8,14},{9,15},{10,... | collective-permute-start | bytes 479240 | tf_op jit(solution)/shard_map/ppermute | solution.py:459
  94.9 15.7 %collective-permute-start.6 = (bf16[624,128]{1,0:T(8,128)(2,1)}, bf16[624,128]{1,0:T(8,128)(2,1)S(1)}, u32[]{:S(2)}, u32[]{:S(2)}) collective-permute-start(bf16[624,128]{1,0:T(8,128)(2,1)} %get-tuple-element.82), channel_id=1, source_target_pairs={{0,4},{1,5},{2,6},{3,7},{4,0},{5,1},{6,2},{7,3},{8,12},{9,13},{10,... | collective-permute-start | bytes 479240 | tf_op jit(solution)/shard_map/ppermute | solution.py:459
  95.8 14.8 %collective-permute-start.8 = (bf16[624,128]{1,0:T(8,128)(2,1)}, bf16[624,128]{1,0:T(8,128)(2,1)S(1)}, u32[]{:S(2)}, u32[]{:S(2)}) collective-permute-start(bf16[624,128]{1,0:T(8,128)(2,1)} %get-tuple-element.84), channel_id=1, source_target_pairs={{0,2},{1,3},{2,4},{3,5},{4,6},{5,7},{6,0},{7,1},{8,10},{9,11},{10,... | collective-permute-start | bytes 479240 | tf_op jit(solution)/shard_map/ppermute | solution.py:459
  99.0 11.6 %copy-start.8 = (bf16[384,128]{1,0:T(8,128)(2,1)}, bf16[384,128]{1,0:T(8,128)(2,1)S(1)}, u32[]{:S(2)}) copy-start(bf16[384,128]{1,0:T(8,128)(2,1)S(1)} %collective-permute-done.3.refs_1_) | copy-start | bytes 294916
  99.0 8.0 %collective-permute-start.7 = (bf16[384,128]{1,0:T(8,128)(2,1)}, bf16[384,128]{1,0:T(8,128)(2,1)S(1)}, u32[]{:S(2)}, u32[]{:S(2)}) collective-permute-start(bf16[384,128]{1,0:T(8,128)(2,1)} %get-tuple-element.83), channel_id=1, source_target_pairs={{0,5},{1,4},{2,7},{3,6},{4,1},{5,0},{6,3},{7,2},{8,13},{9,12},{10,... | collective-permute-start | bytes 294920 | tf_op jit(solution)/shard_map/ppermute | solution.py:459
  100.2 10.3 %copy-start.9 = (bf16[384,128]{1,0:T(8,128)(2,1)}, bf16[384,128]{1,0:T(8,128)(2,1)S(1)}, u32[]{:S(2)}) copy-start(bf16[384,128]{1,0:T(8,128)(2,1)S(1)} %collective-permute-done.5.refs_3_) | copy-start | bytes 294916
  100.2 10.3 %collective-permute-start.9 = (bf16[384,128]{1,0:T(8,128)(2,1)}, bf16[384,128]{1,0:T(8,128)(2,1)S(1)}, u32[]{:S(2)}, u32[]{:S(2)}) collective-permute-start(bf16[384,128]{1,0:T(8,128)(2,1)} %get-tuple-element.85), channel_id=1, source_target_pairs={{0,3},{1,2},{2,5},{3,4},{4,7},{5,6},{6,1},{7,0},{8,11},{9,10},{10,... | collective-permute-start | bytes 294920 | tf_op jit(solution)/shard_map/ppermute | solution.py:459
  107.0 3.6 %copy-start.10 = (bf16[384,128]{1,0:T(8,128)(2,1)}, bf16[384,128]{1,0:T(8,128)(2,1)S(1)}, u32[]{:S(2)}) copy-start(bf16[384,128]{1,0:T(8,128)(2,1)S(1)} %collective-permute-done.7.refs_5_) | copy-start | bytes 294916
  (6 other events, 4.0 us)

commit v3 on v2

--- a/solution.py
+++ b/solution.py
@@ -51,7 +51,8 @@
 
 def route(place, index, way=1):
     blocks = ROUTES // 2
-    return ((place // 2 + blocks + way * (index // 2)) % blocks) * 2 + (place + index) % 2
+    shift = (index // 2 + blocks // 2 * (index % 2)) % blocks
+    return ((place // 2 + blocks + way * shift) % blocks) * 2 + (place + index) % 2
 
 
 def pack_kernel(half_heads, slots, place_ref, iq_ref, ik_ref, iv_ref, ic_ref, *refs):

time: 117 us -> 114 us (0.974)
  waiting for transfers between devices: 29.4 us -> 24.4 us
  starting transfers between devices: 40.9 us -> 42.5 us
    ppermute x10, waiting for transfers between devices: 8.6 us -> 5.06 us  [step_back(): return lax.ppermute(operand, ('blk', 'uly'), pairs)]
    ppermute x10, starting transfers between devices: 11.4 us -> 13 us  [step_back(): return lax.ppermute(operand, ('blk', 'uly'), pairs)]
    all_to_all x4, waiting for transfers between devices: 20.8 us -> 19.3 us  [exchange(): return lax.all_to_all(operand, axes, 0, 0, tiled=True)]
  transfers between devices with their start and end apart: 14 -> 14, of which waited for: 7 -> 6; matrix products, arithmetic and copies ran while one was open for 1% -> 1% of each run, Pallas kernels for 29% -> 30%
where the time goes in v3:
time: 114 us; the launch traced here: 112 us
  starting transfers between devices  42.5 us (37%)
  Pallas kernels  41.2 us (36%)
  waiting for transfers between devices  24.4 us (21%)
  local copies, waits for them, and re-layouts  3.67 us (3%)
    pallas_call x7, Pallas kernels, call(): pl.pallas_call(kernel, in_specs=[pl.BlockSpec(memory_space=pltpu.SMEM)] *...  41.2 us
    all_to_all x4, starting transfers between devices, exchange(): return lax.all_to_all(operand, axes, 0, 0, tiled=True)  29.5 us
    all_to_all x4, waiting for transfers between devices, exchange(): return lax.all_to_all(operand, axes, 0, 0, tiled=True)  19.3 us
    ppermute x10, starting transfers between devices, step_back(): return lax.ppermute(operand, ('blk', 'uly'), pairs)  13 us
    ppermute x10, waiting for transfers between devices, step_back(): return lax.ppermute(operand, ('blk', 'uly'), pairs)  5.06 us
    unnamed x32, local copies, waits for them, and re-layouts  2.42 us
  transfers between devices with their start and end apart: 14, of which 6 were waited for; matrix products, arithmetic and copies ran while one was open for 1% of the time, Pallas kernels for 30%

profile of v3, /device:TPU:1, one launch (start us, length us, event | category | flops | bytes accessed | tf_op | source)
XLA Modules:
  0.0 112.5 jit_solution(7674374486022936866)
XLA Ops:
  0.7 3.3 %pack.3 = bf16[8,768,128]{2,1,0:T(8,128)(2,1)} custom-call(s32[1]{0:T(128)} %bitcast.place_ref.refs_4_, bf16[128,2432]{1,0:T(8,128)(2,1)} %bitcast.15, bf16[128,2432]{1,0:T(8,128)(2,1)} %bitcast.17, bf16[128,2432]{1,0:T(8,128)(2,1)} %bitcast.19, bf16[128,2432]{1,0:T(8,128)(2,1)} %bitcast.21), custom_call_target="tpu_custom_call" | custom-call | tf_op jit(solution)/shard_map/pack/pallas_call | solution.py:377
  3.9 6.0 %all-to-all-start = ((bf16[8,768,128]{2,1,0:T(8,128)(2,1)}), bf16[8,768,128]{2,1,0:T(8,128)(2,1)S(1)}, u32[]{:S(2)}, u32[]{:S(2)}) async-start(bf16[8,768,128]{2,1,0:T(8,128)(2,1)} %pack.3), calls=%async_computation | async-start | bytes 3145728 | tf_op jit(solution)/shard_map/all_to_all | solution.py:389
  10.5 3.1 %pack.2 = (bf16[8,512,128]{2,1,0:T(8,128)(2,1)}, bf16[32,1280]{1,0:T(8,128)(2,1)}, f32[5,2,128]{2,1,0:T(2,128)}) custom-call(s32[1]{0:T(128)} %bitcast.place_ref.refs_4_, bf16[128,2432]{1,0:T(8,128)(2,1)} %bitcast.16, bf16[128,2432]{1,0:T(8,128)(2,1)} %bitcast.18, bf16[128,2432]{1,0:T(8,128)(2,1)} %bitcast.20, bf16[128,2432]{1,0:T(8,128)(2,1)} %bitcast.22, ...), custom_call_target="tpu_custom_call" | custom-call | tf_op jit(solution)/shard_map/pack/pallas_call | solution.py:377
  13.7 19.3 %all-to-all-done.refs_0_ = bf16[8,768,128]{2,1,0:T(8,128)(2,1)S(1)} async-done(((bf16[8,768,128]{2,1,0:T(8,128)(2,1)}), bf16[8,768,128]{2,1,0:T(8,128)(2,1)S(1)}, u32[]{:S(2)}, u32[]{:S(2)}) %all-to-all-start) | async-done | bytes 1572896 | tf_op jit(solution)/shard_map/all_to_all | solution.py:389
  33.0 3.6 %all-to-all-start.1 = ((bf16[8,512,128]{2,1,0:T(8,128)(2,1)}), bf16[8,512,128]{2,1,0:T(8,128)(2,1)S(1)}, u32[]{:S(2)}, u32[]{:S(2)}) async-start(bf16[8,512,128]{2,1,0:T(8,128)(2,1)} %get-tuple-element.56), calls=%async_computation.1 | async-start | bytes 2097152 | tf_op jit(solution)/shard_map/all_to_all | solution.py:389
  36.5 15.3 %attend.2 = (bf16[8,576,128]{2,1,0:T(8,128)(2,1)}, bf16[144,128]{1,0:T(8,128)(2,1)}, f32[8,128]{1,0:T(8,128)}) custom-call(bf16[8,768,128]{2,1,0:T(8,128)(2,1)} %copy-done.2, bf16[32,1280]{1,0:T(8,128)(2,1)} %get-tuple-element.57.refs_1_, f32[2,128]{1,0:T(2,128)} %reshape.19.refs_2_, f32[5,2,128]{2,1,0:T(2,128)} %get-tuple-element.58.refs_3_), custom_call_target="tpu_custom_call" | custom-call | flops 10277093376 | bytes 2752512 | tf_op jit(solution)/shard_map/attend/pallas_call | solution.py:377
  51.8 5.1 %all-to-all-start.2 = ((bf16[8,576,128]{2,1,0:T(8,128)(2,1)}), bf16[8,576,128]{2,1,0:T(8,128)(2,1)S(1)}, u32[]{:S(2)}, u32[]{:S(2)}) async-start(bf16[8,576,128]{2,1,0:T(8,128)(2,1)} %get-tuple-element.75), calls=%async_computation.2 | async-start | bytes 2359296 | tf_op jit(solution)/shard_map/all_to_all | solution.py:389
  56.9 10.6 %attend.3 = (bf16[624,128]{1,0:T(8,128)(2,1)}, bf16[384,128]{1,0:T(8,128)(2,1)}, bf16[624,128]{1,0:T(8,128)(2,1)}, bf16[384,128]{1,0:T(8,128)(2,1)}, bf16[624,12...) custom-call(bf16[8,512,128]{2,1,0:T(8,128)(2,1)} %copy-done.3, ...), custom_call_target="tpu_custom_call" | custom-call | flops 6851395584 | bytes 1835008 | tf_op jit(solution)/shard_map/attend/pallas_call | solution.py:377
  67.5 1.5 %collective-permute-start.2 = (bf16[16,128]{1,0:T(8,128)(2,1)}, bf16[16,128]{1,0:T(8,128)(2,1)S(1)}, u32[]{:S(2)}, u32[]{:S(2)}) collective-permute-start(bf16[16,128]{1,0:T(8,128)(2,1)} %get-tuple-element.71.refs_0_.refs_8_), channel_id=1, source_target_pairs={{0,2},{1,3},{2,4},{3,5},{4,6},{5,7},{6,0},{7,1},{8,10},{9,11},{10,... | collective-permute-start | bytes 12296 | tf_op jit(solution)/shard_map/ppermute | solution.py:460
  69.0 2.4 %collective-permute-start.1 = (bf16[16,128]{1,0:T(8,128)(2,1)}, bf16[16,128]{1,0:T(8,128)(2,1)S(1)}, u32[]{:S(2)}, u32[]{:S(2)}) collective-permute-start(bf16[16,128]{1,0:T(8,128)(2,1)} %get-tuple-element.71.refs_0_.refs_8_), channel_id=1, source_target_pairs={{0,4},{1,5},{2,6},{3,7},{4,0},{5,1},{6,2},{7,3},{8,12},{9,13},{10,... | collective-permute-start | bytes 12296 | tf_op jit(solution)/shard_map/ppermute | solution.py:460
  71.4 1.2 %collective-permute-start = (bf16[16,128]{1,0:T(8,128)(2,1)}, bf16[16,128]{1,0:T(8,128)(2,1)S(1)}, u32[]{:S(2)}, u32[]{:S(2)}) collective-permute-start(bf16[16,128]{1,0:T(8,128)(2,1)} %get-tuple-element.71.refs_0_.refs_8_), channel_id=1, source_target_pairs={{0,6},{1,7},{2,0},{3,1},{4,2},{5,3},{6,4},{7,5},{8,14},{9,15},{10,... | collective-permute-start | bytes 12296 | tf_op jit(solution)/shard_map/ppermute | solution.py:460
  72.6 0.7 constant_dynamic-slice_fusion.cond_ref
  73.6 0.8 collective-permute-done.refs_1_.refs_9_
  74.9 1.5 %spread.1 = bf16[32,16,128]{2,1,0:T(8,128)(2,1)} custom-call(s32[1]{0:T(128)} %bitcast.place_ref.refs_4_, bf16[1,608]{1,0:T(2,128)(2,1)} %constant_dynamic-slice_fusion.cond_ref, bf16[16,128]{1,0:T(8,128)(2,1)} %get-tuple-element.71.refs_0_.refs_8_, bf16[16,128]{1,0:T(8,128)(2,1)} %copy-done.14, bf16[16,128]{1,0:T(8,128)(2,1)} %copy-done.13, ...), custom_call_target="tpu_custom_call" | custom-call | tf_op jit(solution)/shard_map/spread/pallas_call | solution.py:377
  76.4 14.8 %all-to-all-start.3 = ((bf16[32,16,128]{2,1,0:T(8,128)(2,1)}), bf16[32,16,128]{2,1,0:T(8,128)(2,1)S(1)}, u32[]{:S(2)}, u32[]{:S(2)}) async-start(bf16[32,16,128]{2,1,0:T(8,128)(2,1)} %spread.1), calls=%async_computation.3 | async-start | bytes 262144 | tf_op jit(solution)/shard_map/all_to_all | solution.py:389
  91.3 1.6 %collective-permute-start.3 = (bf16[384,128]{1,0:T(8,128)(2,1)}, bf16[384,128]{1,0:T(8,128)(2,1)S(1)}, u32[]{:S(2)}, u32[]{:S(2)}) collective-permute-start(bf16[384,128]{1,0:T(8,128)(2,1)} %get-tuple-element.79), channel_id=1, source_target_pairs={{0,5},{1,4},{2,7},{3,6},{4,1},{5,0},{6,3},{7,2},{8,13},{9,12},{10,... | collective-permute-start | bytes 294920 | tf_op jit(solution)/shard_map/ppermute | solution.py:460
  92.9 2.3 %collective-permute-start.5 = (bf16[384,128]{1,0:T(8,128)(2,1)}, bf16[384,128]{1,0:T(8,128)(2,1)S(1)}, u32[]{:S(2)}, u32[]{:S(2)}) collective-permute-start(bf16[384,128]{1,0:T(8,128)(2,1)} %get-tuple-element.81), channel_id=1, source_target_pairs={{0,3},{1,2},{2,5},{3,4},{4,7},{5,6},{6,1},{7,0},{8,11},{9,10},{10,... | collective-permute-start | bytes 294920 | tf_op jit(solution)/shard_map/ppermute | solution.py:460
  95.2 0.9 collective-permute-start.4
  96.7 1.6 %collective-permute-done.3.refs_1_ = bf16[384,128]{1,0:T(8,128)(2,1)S(1)} collective-permute-done((bf16[384,128]{1,0:T(8,128)(2,1)}, bf16[384,128]{1,0:T(8,128)(2,1)S(1)}, u32[]{:S(2)}, u32[]{:S(2)}) %collective-permute-start.3) | collective-permute-done | bytes 98336 | tf_op jit(solution)/shard_map/ppermute | solution.py:460
  98.9 2.1 %collective-permute-done.5.refs_3_ = bf16[384,128]{1,0:T(8,128)(2,1)S(1)} collective-permute-done((bf16[384,128]{1,0:T(8,128)(2,1)}, bf16[384,128]{1,0:T(8,128)(2,1)S(1)}, u32[]{:S(2)}, u32[]{:S(2)}) %collective-permute-start.5) | collective-permute-done | bytes 98336 | tf_op jit(solution)/shard_map/ppermute | solution.py:460
  101.0 2.0 %collective-permute-start.9 = (bf16[384,128]{1,0:T(8,128)(2,1)}, bf16[384,128]{1,0:T(8,128)(2,1)S(1)}, u32[]{:S(2)}, u32[]{:S(2)}) collective-permute-start(bf16[384,128]{1,0:T(8,128)(2,1)} %get-tuple-element.85), channel_id=1, source_target_pairs={{0,7},{1,6},{2,1},{3,0},{4,3},{5,2},{6,5},{7,4},{8,15},{9,14},{10,... | collective-permute-start | bytes 294920 | tf_op jit(solution)/shard_map/ppermute | solution.py:460
  102.9 0.7 copy-done.4
  103.6 3.2 %modulation.1 = f32[608,1216]{1,0:T(8,128)} custom-call(bf16[32,16,128]{2,1,0:T(8,128)(2,1)} %copy-done.4), custom_call_target="tpu_custom_call" | custom-call | tf_op jit(solution)/shard_map/modulation/pallas_call | solution.py:377
  108.2 4.2 %unpack.1 = (bf16[128,2432]{1,0:T(8,128)(2,1)}, bf16[128,2432]{1,0:T(8,128)(2,1)}, bf16[128,2432]{1,0:T(8,128)(2,1)}, bf16[32,1216]{1,0:T(8,128)(2,1)}, bf16[32,...) custom-call(s32[1]{0:T(128)} %bitcast.place_ref.refs_4_, bf16[8,576,128]{2,1,0:T(8,128)(2,1)} %copy-done.1, ...), custom_call_target="tpu_custom_call" | custom-call | tf_op jit(solution)/shard_map/unpack/pallas_call | solution.py:377
  (45 shorter events, 4.1 us)
Async XLA Ops:
  0.6 71.9 %copy-start = (bf16[1,2432]{1,0:T(2,128)(2,1)S(1)}, bf16[1,2432]{1,0:T(2,128)(2,1)}, u32[]{:S(2)}) copy-start(bf16[1,2432]{1,0:T(2,128)(2,1)} %param.22) | copy-start | bytes 14596
  3.9 6.0 %copy-start.15 = (f32[4,64]{1,0:T(4,128)S(1)}, f32[4,64]{1,0:T(4,128)}, u32[]{:S(2)}) copy-start(f32[4,64]{1,0:T(4,128)} %param.23) | copy-start | bytes 3076
  3.9 29.0 %all-to-all-start = ((bf16[8,768,128]{2,1,0:T(8,128)(2,1)}), bf16[8,768,128]{2,1,0:T(8,128)(2,1)S(1)}, u32[]{:S(2)}, u32[]{:S(2)}) async-start(bf16[8,768,128]{2,1,0:T(8,128)(2,1)} %pack.3), calls=%async_computation | async-start | bytes 3145728 | tf_op jit(solution)/shard_map/all_to_all | solution.py:389
  33.0 3.6 %copy-start.2 = (bf16[8,768,128]{2,1,0:T(8,128)(2,1)}, bf16[8,768,128]{2,1,0:T(8,128)(2,1)S(1)}, u32[]{:S(2)}) copy-start(bf16[8,768,128]{2,1,0:T(8,128)(2,1)S(1)} %all-to-all-done.refs_0_) | copy-start | bytes 4718596
  33.0 18.9 %all-to-all-start.1 = ((bf16[8,512,128]{2,1,0:T(8,128)(2,1)}), bf16[8,512,128]{2,1,0:T(8,128)(2,1)S(1)}, u32[]{:S(2)}, u32[]{:S(2)}) async-start(bf16[8,512,128]{2,1,0:T(8,128)(2,1)} %get-tuple-element.56), calls=%async_computation.1 | async-start | bytes 2097152 | tf_op jit(solution)/shard_map/all_to_all | solution.py:389
  51.8 5.1 %copy-start.3 = (bf16[8,512,128]{2,1,0:T(8,128)(2,1)}, bf16[8,512,128]{2,1,0:T(8,128)(2,1)S(1)}, u32[]{:S(2)}) copy-start(bf16[8,512,128]{2,1,0:T(8,128)(2,1)S(1)} %all-to-all-done.1.refs_0_) | copy-start | bytes 3145732
  51.8 24.6 %all-to-all-start.2 = ((bf16[8,576,128]{2,1,0:T(8,128)(2,1)}), bf16[8,576,128]{2,1,0:T(8,128)(2,1)S(1)}, u32[]{:S(2)}, u32[]{:S(2)}) async-start(bf16[8,576,128]{2,1,0:T(8,128)(2,1)} %get-tuple-element.75), calls=%async_computation.2 | async-start | bytes 2359296 | tf_op jit(solution)/shard_map/all_to_all | solution.py:389
  67.5 5.7 %collective-permute-start.2 = (bf16[16,128]{1,0:T(8,128)(2,1)}, bf16[16,128]{1,0:T(8,128)(2,1)S(1)}, u32[]{:S(2)}, u32[]{:S(2)}) collective-permute-start(bf16[16,128]{1,0:T(8,128)(2,1)} %get-tuple-element.71.refs_0_.refs_8_), channel_id=1, source_target_pairs={{0,2},{1,3},{2,4},{3,5},{4,6},{5,7},{6,0},{7,1},{8,10},{9,11},{10,... | collective-permute-start | bytes 12296 | tf_op jit(solution)/shard_map/ppermute | solution.py:460
  69.0 4.6 %collective-permute-start.1 = (bf16[16,128]{1,0:T(8,128)(2,1)}, bf16[16,128]{1,0:T(8,128)(2,1)S(1)}, u32[]{:S(2)}, u32[]{:S(2)}) collective-permute-start(bf16[16,128]{1,0:T(8,128)(2,1)} %get-tuple-element.71.refs_0_.refs_8_), channel_id=1, source_target_pairs={{0,4},{1,5},{2,6},{3,7},{4,0},{5,1},{6,2},{7,3},{8,12},{9,13},{10,... | collective-permute-start | bytes 12296 | tf_op jit(solution)/shard_map/ppermute | solution.py:460
  71.4 3.0 %collective-permute-start = (bf16[16,128]{1,0:T(8,128)(2,1)}, bf16[16,128]{1,0:T(8,128)(2,1)S(1)}, u32[]{:S(2)}, u32[]{:S(2)}) collective-permute-start(bf16[16,128]{1,0:T(8,128)(2,1)} %get-tuple-element.71.refs_0_.refs_8_), channel_id=1, source_target_pairs={{0,6},{1,7},{2,0},{3,1},{4,2},{5,3},{6,4},{7,5},{8,14},{9,15},{10,... | collective-permute-start | bytes 12296 | tf_op jit(solution)/shard_map/ppermute | solution.py:460
  73.2 1.1 %copy-start.12 = (bf16[16,128]{1,0:T(8,128)(2,1)}, bf16[16,128]{1,0:T(8,128)(2,1)S(1)}, u32[]{:S(2)}) copy-start(bf16[16,128]{1,0:T(8,128)(2,1)S(1)} %collective-permute-done.2.refs_3_.refs_11_) | copy-start | bytes 12292
  73.6 0.8 copy-start.13
  76.4 30.3 %copy-start.1 = (bf16[8,576,128]{2,1,0:T(8,128)(2,1)}, bf16[8,576,128]{2,1,0:T(8,128)(2,1)S(1)}, u32[]{:S(2)}) copy-start(bf16[8,576,128]{2,1,0:T(8,128)(2,1)S(1)} %all-to-all-done.2.first_ref) | copy-start | bytes 3538948
  76.4 26.5 %all-to-all-start.3 = ((bf16[32,16,128]{2,1,0:T(8,128)(2,1)}), bf16[32,16,128]{2,1,0:T(8,128)(2,1)S(1)}, u32[]{:S(2)}, u32[]{:S(2)}) async-start(bf16[32,16,128]{2,1,0:T(8,128)(2,1)} %spread.1), calls=%async_computation.3 | async-start | bytes 262144 | tf_op jit(solution)/shard_map/all_to_all | solution.py:389
  91.3 7.0 %collective-permute-start.3 = (bf16[384,128]{1,0:T(8,128)(2,1)}, bf16[384,128]{1,0:T(8,128)(2,1)S(1)}, u32[]{:S(2)}, u32[]{:S(2)}) collective-permute-start(bf16[384,128]{1,0:T(8,128)(2,1)} %get-tuple-element.79), channel_id=1, source_target_pairs={{0,5},{1,4},{2,7},{3,6},{4,1},{5,0},{6,3},{7,2},{8,13},{9,12},{10,... | collective-permute-start | bytes 294920 | tf_op jit(solution)/shard_map/ppermute | solution.py:460
  92.9 8.1 %collective-permute-start.5 = (bf16[384,128]{1,0:T(8,128)(2,1)}, bf16[384,128]{1,0:T(8,128)(2,1)S(1)}, u32[]{:S(2)}, u32[]{:S(2)}) collective-permute-start(bf16[384,128]{1,0:T(8,128)(2,1)} %get-tuple-element.81), channel_id=1, source_target_pairs={{0,3},{1,2},{2,5},{3,4},{4,7},{5,6},{6,1},{7,0},{8,11},{9,10},{10,... | collective-permute-start | bytes 294920 | tf_op jit(solution)/shard_map/ppermute | solution.py:460
  95.2 11.6 %collective-permute-start.4 = (bf16[624,128]{1,0:T(8,128)(2,1)}, bf16[624,128]{1,0:T(8,128)(2,1)S(1)}, u32[]{:S(2)}, u32[]{:S(2)}) collective-permute-start(bf16[624,128]{1,0:T(8,128)(2,1)} %get-tuple-element.80), channel_id=1, source_target_pairs={{0,6},{1,7},{2,0},{3,1},{4,2},{5,3},{6,4},{7,5},{8,14},{9,15},{10,... | collective-permute-start | bytes 479240 | tf_op jit(solution)/shard_map/ppermute | solution.py:460
  96.1 10.7 %collective-permute-start.6 = (bf16[624,128]{1,0:T(8,128)(2,1)}, bf16[624,128]{1,0:T(8,128)(2,1)S(1)}, u32[]{:S(2)}, u32[]{:S(2)}) collective-permute-start(bf16[624,128]{1,0:T(8,128)(2,1)} %get-tuple-element.82), channel_id=1, source_target_pairs={{0,4},{1,5},{2,6},{3,7},{4,0},{5,1},{6,2},{7,3},{8,12},{9,13},{10,... | collective-permute-start | bytes 479240 | tf_op jit(solution)/shard_map/ppermute | solution.py:460
  96.7 10.4 %collective-permute-start.8 = (bf16[624,128]{1,0:T(8,128)(2,1)}, bf16[624,128]{1,0:T(8,128)(2,1)S(1)}, u32[]{:S(2)}, u32[]{:S(2)}) collective-permute-start(bf16[624,128]{1,0:T(8,128)(2,1)} %get-tuple-element.84), channel_id=1, source_target_pairs={{0,2},{1,3},{2,4},{3,5},{4,6},{5,7},{6,0},{7,1},{8,10},{9,11},{10,... | collective-permute-start | bytes 479240 | tf_op jit(solution)/shard_map/ppermute | solution.py:460
  98.3 8.8 %copy-start.8 = (bf16[384,128]{1,0:T(8,128)(2,1)}, bf16[384,128]{1,0:T(8,128)(2,1)S(1)}, u32[]{:S(2)}) copy-start(bf16[384,128]{1,0:T(8,128)(2,1)S(1)} %collective-permute-done.3.refs_1_) | copy-start | bytes 294916
  98.3 8.5 %collective-permute-start.7 = (bf16[384,128]{1,0:T(8,128)(2,1)}, bf16[384,128]{1,0:T(8,128)(2,1)S(1)}, u32[]{:S(2)}, u32[]{:S(2)}) collective-permute-start(bf16[384,128]{1,0:T(8,128)(2,1)} %get-tuple-element.83), channel_id=1, source_target_pairs={{0,1},{1,0},{2,3},{3,2},{4,5},{5,4},{6,7},{7,6},{8,9},{9,8},{10,11... | collective-permute-start | bytes 294920 | tf_op jit(solution)/shard_map/ppermute | solution.py:460
  101.0 6.1 %copy-start.9 = (bf16[384,128]{1,0:T(8,128)(2,1)}, bf16[384,128]{1,0:T(8,128)(2,1)S(1)}, u32[]{:S(2)}) copy-start(bf16[384,128]{1,0:T(8,128)(2,1)S(1)} %collective-permute-done.5.refs_3_) | copy-start | bytes 294916
  101.0 5.8 %collective-permute-start.9 = (bf16[384,128]{1,0:T(8,128)(2,1)}, bf16[384,128]{1,0:T(8,128)(2,1)S(1)}, u32[]{:S(2)}, u32[]{:S(2)}) collective-permute-start(bf16[384,128]{1,0:T(8,128)(2,1)} %get-tuple-element.85), channel_id=1, source_target_pairs={{0,7},{1,6},{2,1},{3,0},{4,3},{5,2},{6,5},{7,4},{8,15},{9,14},{10,... | collective-permute-start | bytes 294920 | tf_op jit(solution)/shard_map/ppermute | solution.py:460
  106.8 0.7 copy-start.6
  (6 other events, 3.9 us)
